TPU v7x, 128 devices: a whole 4x4x4 slice. The times are simulated.
128 devices in a mesh: seq: 8 (over x, core), exp: 16 (over y, z).
Axes of the slice: x: 4, y: 4, z: 4, core: 2. Of those that a mesh axis runs over, the one named last changes fastest.
Arguments:
- query_rows: bfloat16 [16, 1536, 4096], P('exp', 'seq'), may hold values from -6 to 6
- key_rows: bfloat16 [16, 1536, 512], P('exp', 'seq'), may hold values from -6 to 6
- value_matrix: bfloat16 [16, 1536, 512], P('exp', 'seq'), may hold values from -6 to 6
- doc_ids: int32 [16, 1536], P('exp'), may hold values from 0 to 7, as said below
- out_weight: bfloat16 [4096, 2048], P(('seq', 'exp')), may hold values from -0.375 to 0.375
- enc_weight: bfloat16 [128, 2048, 1024], P(('seq', 'exp')), may hold values from -0.125 to 0.125
- enc_bias: float32 [128, 1024], P(('seq', 'exp')), may hold values from -3 to 3
- dec_weight: bfloat16 [128, 1024, 2048], P(('seq', 'exp')), may hold values from -0.1875 to 0.1875
- dec_bias: float32 [2048], replicated, may hold values from -3 to 3
- expert_ids: int32 [16, 1536], P('exp', 'seq'), may hold values from 0 to 127
- slot_ids: int32 [16, 1536], P('exp', 'seq'), may hold values from -1 to 2, as said below
Outputs:
- harvested: bfloat16 [16, 1536, 2048], P('exp', 'seq')
- reconstruction: bfloat16 [16, 1536, 2048], P('exp', 'seq')
- error_rows: bfloat16 [16, 1536, 2048], P('exp', 'seq')
- dec_grad: bfloat16 [128, 1024, 2048], P(('seq', 'exp'))
Inputs may be any that keep to these rules, and one draw needn't show every extreme that they name: `doc_ids`: each sequence's numbers start at 0, never fall, and rise by one at each of 7 document starts. `slot_ids`: among one device's tokens, those that name the same expert and are kept hold the slots 0 to n - 1 in some order, n at most 3; -1 marks a token left out. In every draw some expert holds all 3 slots on every device.
All inputs are finite; a program needn't handle non-finite values.
Results may differ from a plain program's by a relative error of at most 0.014.
Values may be sent and summed in bfloat16 or wider, within the bound.
A program may use at most 128 MiB of HBM per device.

v0:
```python
import math

import jax
import jax.numpy as jnp
from jax import lax
from jax.sharding import PartitionSpec as P

HEAD_DIMENSION = 128


masked_score = -1e30


def attend_block(query_block, key_part, value_part, visible, score_scale):
    scores = (
        jnp.einsum("qhd,kd->hqk", query_block, key_part, preferred_element_type=jnp.float32)
        * score_scale
    )
    scores = jnp.where(visible[None, :, :], scores, masked_score)
    highest = jnp.max(scores, axis=2, keepdims=True)
    weights = jnp.exp(scores - highest)
    normed = (weights / jnp.sum(weights, axis=2, keepdims=True)).astype(jnp.bfloat16)
    mixed = jnp.einsum("hqk,kd->qhd", normed, value_part, preferred_element_type=jnp.float32)
    return mixed.astype(jnp.bfloat16)


def shards(
    query_rows,
    key_rows,
    value_matrix,
    doc_ids,
    out_weight,
    enc_weight,
    enc_bias,
    dec_weight,
    dec_bias,
    expert_ids,
    slot_ids,
):
    local_tokens = query_rows.shape[1]
    seq_groups = lax.axis_size("seq")
    exp_groups = lax.axis_size("exp")
    devices_all = seq_groups * exp_groups
    query_heads = query_rows.shape[2] // HEAD_DIMENSION
    kv_heads = key_rows.shape[2] // HEAD_DIMENSION
    heads_here = query_heads // seq_groups
    kv_share = seq_groups // kv_heads
    query_local = query_rows[0].reshape(local_tokens, seq_groups, heads_here * HEAD_DIMENSION)
    paired = jnp.concatenate(
        [
            key_rows[0].reshape(local_tokens, kv_heads, HEAD_DIMENSION),
            value_matrix[0].reshape(local_tokens, kv_heads, HEAD_DIMENSION),
        ],
        axis=2,
    )
    paired = jnp.repeat(paired, kv_share, axis=1)
    query_all, paired_all = (
        lax.all_to_all(query_local, "seq", split_axis=1, concat_axis=0, tiled=True),
        lax.all_to_all(paired, "seq", split_axis=1, concat_axis=0, tiled=True),
    )
    span_length = local_tokens * seq_groups
    query_all = query_all.reshape(span_length, heads_here, HEAD_DIMENSION)
    key_all = paired_all[:, 0, :HEAD_DIMENSION]
    value_all = paired_all[:, 0, HEAD_DIMENSION:]
    doc_row = doc_ids[0]
    positions = jnp.arange(span_length)
    block_rows = 512
    score_scale = 1.0 / math.sqrt(HEAD_DIMENSION)
    pieces_out = []
    for row_start in range(0, span_length, block_rows):
        row_stop = row_start + block_rows
        visible = (positions[row_start:row_stop, None] >= positions[None, :row_stop]) & (
            doc_row[row_start:row_stop, None] == doc_row[None, :row_stop]
        )
        mixed = attend_block(
            query_all[row_start:row_stop],
            key_all[:row_stop],
            value_all[:row_stop],
            visible,
            score_scale,
        )
        pieces_out.append(mixed.reshape(block_rows, heads_here * HEAD_DIMENSION))
    attended = jnp.concatenate(pieces_out, axis=0)
    heads_back = lax.all_to_all(
        attended.reshape(seq_groups, local_tokens, heads_here * HEAD_DIMENSION),
        "seq",
        split_axis=0,
        concat_axis=2,
        tiled=True,
    )
    head_features = heads_back[0]
    projected = jnp.dot(
        head_features,
        lax.all_gather(out_weight, ("seq", "exp"), axis=0, tiled=True),
        preferred_element_type=jnp.float32,
    )
    harvested = projected.astype(jnp.bfloat16)
    local_experts = enc_weight.shape[0]
    experts_all = local_experts * devices_all
    capacity = 2 * local_tokens // experts_all
    model_width = harvested.shape[1]
    expert_here = expert_ids[0]
    slot_here = slot_ids[0]
    kept_token = slot_here >= 0
    slot_count = experts_all * capacity
    target = jnp.where(kept_token, expert_here * capacity + slot_here, slot_count)
    send_rows = (
        jnp.zeros((slot_count, model_width), jnp.bfloat16).at[target].set(harvested, mode="drop")
    )
    send_live = (
        jnp.zeros((slot_count,), jnp.bfloat16)
        .at[target]
        .set(jnp.ones((local_tokens,), jnp.bfloat16), mode="drop")
    )
    arrived, arrived_live = (
        lax.all_to_all(
            send_rows.reshape(devices_all, local_experts, capacity, model_width),
            ("seq", "exp"),
            split_axis=0,
            concat_axis=2,
            tiled=True,
        ),
        lax.all_to_all(
            send_live.reshape(devices_all, local_experts, capacity),
            ("seq", "exp"),
            split_axis=0,
            concat_axis=2,
            tiled=True,
        ),
    )
    slot_total = devices_all * capacity
    slot_rows = arrived.reshape(local_experts, slot_total, model_width)
    slot_live = arrived_live.reshape(local_experts, slot_total)
    centered = (slot_rows.astype(jnp.float32) - dec_bias).astype(jnp.bfloat16)
    pre_act = (
        jnp.einsum("esd,edf->esf", centered, enc_weight, preferred_element_type=jnp.float32)
        + enc_bias[:, None, :]
    )
    latent = jnp.maximum(pre_act, 0.0).astype(jnp.bfloat16)
    rebuilt = (
        jnp.einsum("esf,efd->esd", latent, dec_weight, preferred_element_type=jnp.float32)
        + dec_bias
    ).astype(jnp.bfloat16)
    residue = (rebuilt.astype(jnp.float32) - slot_rows.astype(jnp.float32)).astype(jnp.bfloat16)
    gated = latent * slot_live[:, :, None]
    dec_grad = jnp.einsum(
        "esf,esd->efd", gated, residue, preferred_element_type=jnp.float32
    ).astype(jnp.bfloat16)
    returned = lax.all_to_all(
        rebuilt.reshape(1, local_experts, slot_total, model_width),
        ("seq", "exp"),
        split_axis=2,
        concat_axis=0,
        tiled=True,
    )
    returned = returned.reshape(slot_count, model_width)
    picked_rows = returned[jnp.minimum(target, slot_count - 1)]
    reconstruction = jnp.where(
        kept_token[:, None], picked_rows, dec_bias.astype(jnp.bfloat16)[None, :]
    )
    error_rows = (reconstruction.astype(jnp.float32) - harvested.astype(jnp.float32)).astype(
        jnp.bfloat16
    )
    return (harvested[None], reconstruction[None], error_rows[None], dec_grad)


def solution(mesh):
    return jax.shard_map(
        shards,
        mesh=mesh,
        in_specs=(
            P("exp", "seq", None),
            P("exp", "seq", None),
            P("exp", "seq", None),
            P("exp", None),
            P(("seq", "exp"), None),
            P(("seq", "exp"), None, None),
            P(("seq", "exp"), None),
            P(("seq", "exp"), None, None),
            P(),
            P("exp", "seq"),
            P("exp", "seq"),
        ),
        out_specs=(
            P("exp", "seq", None),
            P("exp", "seq", None),
            P("exp", "seq", None),
            P(("seq", "exp"), None, None),
        ),
        check_vma=False,
    )
```

profile of v0, /device:TPU:1, one launch (start us, length us, event | category | flops | bytes accessed | tf_op | source)
XLA Modules:
  0.0 279.6 jit_solution(2984221756998044651)
XLA Ops:
  7.9 2.1 copy.86
  11.6 5.9 %all-to-all-start.1 = ((bf16[192,8,512]{2,0,1:T(8,128)(2,1)}), bf16[192,8,512]{2,0,1:T(8,128)(2,1)S(1)}, u32[]{:S(2)}, u32[]{:S(2)}) async-start(bf16[192,8,512]{2,0,1:T(8,128)(2,1)} %copy.56), calls=%async_computation.1 | async-start | bytes 3145728 | tf_op jit(solution)/shard_map/all_to_all | solution.py:58
  19.8 19.7 %all-to-all-done.1 = bf16[192,8,512]{2,0,1:T(8,128)(2,1)S(1)} async-done(((bf16[192,8,512]{2,0,1:T(8,128)(2,1)}), bf16[192,8,512]{2,0,1:T(8,128)(2,1)S(1)}, u32[]{:S(2)}, u32[]{:S(2)}) %all-to-all-start.1) | async-done | bytes 1572896 | tf_op jit(solution)/shard_map/all_to_all | solution.py:58
  40.5 5.3 %all-to-all-start = ((bf16[192,8,256]{2,0,1:T(8,128)(2,1)}), bf16[192,8,256]{2,0,1:T(8,128)(2,1)}, u32[]{:S(2)}, u32[]{:S(2)}) async-start(bf16[192,8,256]{2,0,1:T(8,128)(2,1)} %bitcast), calls=%async_computation | async-start | bytes 1572864 | tf_op jit(solution)/shard_map/all_to_all | solution.py:59
  49.1 13.0 %all-to-all-done = bf16[192,8,256]{2,0,1:T(8,128)(2,1)} async-done(((bf16[192,8,256]{2,0,1:T(8,128)(2,1)}), bf16[192,8,256]{2,0,1:T(8,128)(2,1)}, u32[]{:S(2)}, u32[]{:S(2)}) %all-to-all-start) | async-done | bytes 786464 | tf_op jit(solution)/shard_map/all_to_all | solution.py:59
  62.2 7.3 %fusion.61 = (f32[4,512]{1,0:T(4,128)S(1)}, f32[4,512,1024]{1,2,0:T(8,128)}) fusion(pred[512,1024]{0,1:T(8,128)(4,1)S(1)} %copy-done.3, bf16[512,4,128]{2,1,0:T(4,128)(2,1)S(1)} %get-tuple-element.7, bf16[1536,1,256]{2,0,1:T(8,128)(2,1)} %bitcast.3), kind=kOutput, calls=%fused_computation.92 | convolution fusion | flops 545260544 | bytes 9707520 | tf_op jit(solution)/shard_map/sub | solution.py:21
  69.5 4.2 %fusion.28 = bf16[128,4,512]{2,0,1:T(8,128)(2,1)S(1)} fusion(f32[4,512,1024]{1,2,0:T(8,128)} %get-tuple-element.15, f32[4,512]{1,0:T(4,128)S(1)} %get-tuple-element.14, bf16[1536,1,256]{2,0,1:T(8,128)(2,1)} %bitcast.3), kind=kOutput, calls=%fused_computation.47 | convolution fusion | flops 541327360 | bytes 9183232 | tf_op jit(solution)/shard_map/hqk,kd->qhd/dot_general | solution.py:23
  75.5 2.1 fusion.66
  79.3 2.8 fusion.36
  82.1 10.3 %fusion.60 = (f32[4,512]{1,0:T(4,128)S(1)}, f32[4,512,1536]{1,2,0:T(8,128)}) fusion(f32[1536,512,4]{1,0,2:T(8,128)S(1)} %fusion.36, pred[512,1536]{0,1:T(8,128)(4,1)} %fusion.18), kind=kOutput, calls=%fused_computation.91 | output fusion | flops 18875904 | bytes 25960448 | tf_op jit(solution)/shard_map/sub | solution.py:21
  92.5 6.1 %fusion.29 = bf16[128,4,512]{2,0,1:T(8,128)(2,1)S(1)} fusion(f32[4,512,1536]{1,2,0:T(8,128)} %get-tuple-element.13, f32[4,512]{1,0:T(4,128)S(1)} %get-tuple-element.12, bf16[1536,1,256]{2,0,1:T(8,128)(2,1)} %bitcast.3), kind=kOutput, calls=%fused_computation.48 | convolution fusion | flops 811859968 | bytes 13508608 | tf_op jit(solution)/shard_map/hqk,kd->qhd/dot_general | solution.py:23
  100.1 5.2 %all-to-all-start.2 = ((bf16[8,192,512]{2,1,0:T(8,128)(2,1)}), bf16[8,192,512]{2,1,0:T(8,128)(2,1)S(1)}, u32[]{:S(2)}, u32[]{:S(2)}) async-start(bf16[8,192,512]{2,1,0:T(8,128)(2,1)} %bitcast.33), calls=%async_computation.2 | async-start | bytes 3145728 | tf_op jit(solution)/shard_map/all_to_all | solution.py:84
  105.3 20.7 %all-to-all-done.2 = bf16[8,192,512]{2,1,0:T(8,128)(2,1)S(1)} async-done(((bf16[8,192,512]{2,1,0:T(8,128)(2,1)}), bf16[8,192,512]{2,1,0:T(8,128)(2,1)S(1)}, u32[]{:S(2)}, u32[]{:S(2)}) %all-to-all-start.2) | async-done | bytes 1572896 | tf_op jit(solution)/shard_map/all_to_all | solution.py:84
  126.2 8.6 %convolution_convert_fusion = bf16[192,2048]{1,0:T(8,128)(2,1)} fusion(bf16[192,4096]{1,0:T(8,128)(2,1)S(1)} %bitcast.149, bf16[4096,2048]{1,0:T(8,128)(2,1)} %all-gather.2.cloned.1.call-done), kind=kOutput, calls=%fused_computation.36 | convolution fusion | flops 3221618688 | bytes 19136512 | tf_op jit(solution)/shard_map/dot_general | solution.py:92
  134.8 2.9 %scatter_custom_fusion = bf16[384,2048]{1,0:T(8,128)(2,1)S(1)} fusion(s32[192]{0:T(256)S(1)} %bitcast.160, bf16[192,2048]{1,0:T(8,128)(2,1)} %convolution_convert_fusion, bf16[]{:T(256)} %constant.0.clone.1), kind=kCustom, calls=%fused_computation.54 | custom fusion | bytes 1573376 | tf_op jit(solution)/shard_map/scatter | solution.py:108
  137.7 2.3 reshape.427
  140.0 10.5 %all-to-all-start.3 = ((bf16[128,1,3,2048]{3,2,1,0:T(4,128)(2,1)}), bf16[128,1,3,2048]{3,2,1,0:T(4,128)(2,1)S(1)}, u32[]{:S(2)}, u32[]{:S(2)}) async-start(bf16[128,1,3,2048]{3,2,1,0:T(4,128)(2,1)} %bitcast.144), calls=%async_computation.3 | async-start | bytes 4194304 | tf_op jit(solution)/shard_map/all_to_all | solution.py:116
  153.1 26.8 %all-to-all-done.3 = bf16[128,1,3,2048]{3,2,1,0:T(4,128)(2,1)S(1)} async-done(((bf16[128,1,3,2048]{3,2,1,0:T(4,128)(2,1)}), bf16[128,1,3,2048]{3,2,1,0:T(4,128)(2,1)S(1)}, u32[]{:S(2)}, u32[]{:S(2)}) %all-to-all-start.3) | async-done | bytes 1572896 | tf_op jit(solution)/shard_map/all_to_all | solution.py:116
  180.0 4.9 %all-to-all-start.5 = ((bf16[128,1,3]{2,1,0:T(2,128)(2,1)}), bf16[128,1,3]{2,1,0:T(2,128)(2,1)S(1)}, u32[]{:S(2)}, u32[]{:S(2)}) async-start(bf16[128,1,3]{2,1,0:T(2,128)(2,1)} %reshape.464), calls=%async_computation.5 | async-start | bytes 131072 | tf_op jit(solution)/shard_map/all_to_all | solution.py:123
  184.9 2.5 subtract_convert_fusion
  187.4 5.4 %convert_element_type.100 = bf16[384,2048]{1,0:T(8,128)(2,1)} reshape(bf16[128,1,3,2048]{3,2,1,0:T(4,128)(2,1)} %subtract_convert_fusion) | data formatting | bytes 3145728 | tf_op jit(solution)/shard_map/convert_element_type | solution.py:134
  192.8 4.6 %maximum_convert_fusion = bf16[384,1024]{1,0:T(8,128)(2,1)S(1)} fusion(bf16[384,2048]{1,0:T(8,128)(2,1)} %convert_element_type.100, bf16[1,2048,1024]{2,1,0:T(8,128)(2,1)} %param.16, f32[1024]{0:T(1024)S(1)} %bitcast.162), kind=kOutput, calls=%fused_computation.45 | convolution fusion | flops 1611792384 | bytes 6557696 | tf_op jit(solution)/shard_map/esd,edf->esf/dot_general | solution.py:136
  197.4 1.8 add_convert_fusion
  200.4 4.1 %copy.108 = bf16[1,1,384,2048]{3,1,0,2:T(2,128)(2,1)} copy(bf16[1,1,384,2048]{3,2,1,0:T(8,128)(2,1)S(1)} %bitcast.150) | data formatting | bytes 3145728 | tf_op jit(solution)/shard_map/reshape | solution.py:150
  205.0 12.6 %reduce.4 = bf16[384,2048]{1,0:T(8,128)(2,1)} reduce(bf16[384,1,1,2048]{3,2,1,0:T(2,128)(2,1)} %bitcast.142, bf16[]{:T(256)} %broadcast.281), dimensions={1,2}, to_apply=%bitcast.140.reduce_sub_computation | reduce | bytes 3145730
  217.6 4.5 %reshape.472 = bf16[128,2,3072]{2,1,0:T(2,128)(2,1)} reshape(bf16[384,2048]{1,0:T(8,128)(2,1)} %reduce.4) | data formatting | bytes 3145728
  222.1 10.2 %all-to-all-start.4 = ((bf16[128,2,3072]{2,1,0:T(2,128)(2,1)}), bf16[128,2,3072]{2,1,0:T(2,128)(2,1)}, u32[]{:S(2)}, u32[]{:S(2)}) async-start(bf16[128,2,3072]{2,1,0:T(2,128)(2,1)} %reshape.472), calls=%async_computation.4 | async-start | bytes 3145728 | tf_op jit(solution)/shard_map/all_to_all | solution.py:149
  232.8 2.7 reshape.433
  235.5 6.8 %convert_bitcast_fusion = bf16[1,1024,2048]{2,1,0:T(8,128)(2,1)} fusion(f32[384,2048]{1,0:T(8,128)} %reshape.433, bf16[384,2048]{1,0:T(8,128)(2,1)} %copy-done.1, bf16[384,1024]{1,0:T(8,128)(2,1)S(1)} %maximum_convert_fusion, bf16[384]{0:T(512)(128)(2,1)S(1)} %mul.67), kind=kOutput, calls=%fused_computation.23 | convolution fusion | flops 1615462400 | bytes 9700096 | tf_op jit(solution)/shard_map/esf,esd->efd/dot_general | solution.py:146
  242.3 13.7 %all-to-all-done.4 = bf16[128,2,3072]{2,1,0:T(2,128)(2,1)} async-done(((bf16[128,2,3072]{2,1,0:T(2,128)(2,1)}), bf16[128,2,3072]{2,1,0:T(2,128)(2,1)}, u32[]{:S(2)}, u32[]{:S(2)}) %all-to-all-start.4) | async-done | bytes 1572896 | tf_op jit(solution)/shard_map/all_to_all | solution.py:149
  256.0 10.4 %reshape.473 = bf16[384,1,1,2048]{3,2,1,0:T(2,128)(2,1)} reshape(bf16[128,2,3072]{2,1,0:T(2,128)(2,1)} %all-to-all-done.4) | data formatting | bytes 3145728
  266.3 2.8 %copy.107 = bf16[1,1,384,2048]{3,2,0,1:T(8,128)(2,1)S(1)} copy(bf16[1,1,384,2048]{3,1,0,2:T(2,128)(2,1)} %bitcast.143) | data formatting | bytes 3145728
  (68 shorter events, 22.1 us)
Async XLA Ops:
  7.2 119.1 %all-gather.2.cloned.1.call-start = ((), (), s32[]{:S(2)}) async-start(), calls=%async_computation.6 | async-start | bytes 16908288 | tf_op jit(solution)/shard_map/all_gather | solution.py:94
  10.0 7.6 %copy-start.4 = (bf16[1,192,512]{2,1,0:T(8,128)(2,1)S(1)}, bf16[1,192,512]{2,1,0:T(8,128)(2,1)}, u32[]{:S(2)}) copy-start(bf16[1,192,512]{2,1,0:T(8,128)(2,1)} %param.13) | copy-start | bytes 589828
  10.0 7.7 %copy-start.5 = (bf16[1,192,512]{2,1,0:T(8,128)(2,1)S(1)}, bf16[1,192,512]{2,1,0:T(8,128)(2,1)}, u32[]{:S(2)}) copy-start(bf16[1,192,512]{2,1,0:T(8,128)(2,1)} %param.12) | copy-start | bytes 589828
  11.6 6.3 %copy-start.6 = (s32[1,1536]{1,0:T(1,128)S(1)}, s32[1,1536]{1,0:T(1,128)}, u32[]{:S(2)}) copy-start(s32[1,1536]{1,0:T(1,128)} %param.14) | copy-start | bytes 18436
  11.6 6.7 %slice-start = ((s32[1,1536]{1,0:T(1,128)}), s32[1,1024]{1,0:T(1,128)S(1)}, s32[]{:S(2)}) async-start(s32[1,1536]{1,0:T(1,128)} %param.14), calls=%async_computation.7 | async-start | bytes 8192 | tf_op jit(solution)/shard_map/slice | solution.py:73
  11.6 27.9 %all-to-all-start.1 = ((bf16[192,8,512]{2,0,1:T(8,128)(2,1)}), bf16[192,8,512]{2,0,1:T(8,128)(2,1)S(1)}, u32[]{:S(2)}, u32[]{:S(2)}) async-start(bf16[192,8,512]{2,0,1:T(8,128)(2,1)} %copy.56), calls=%async_computation.1 | async-start | bytes 3145728 | tf_op jit(solution)/shard_map/all_to_all | solution.py:58
  40.5 21.7 %all-to-all-start = ((bf16[192,8,256]{2,0,1:T(8,128)(2,1)}), bf16[192,8,256]{2,0,1:T(8,128)(2,1)}, u32[]{:S(2)}, u32[]{:S(2)}) async-start(bf16[192,8,256]{2,0,1:T(8,128)(2,1)} %bitcast), calls=%async_computation | async-start | bytes 1572864 | tf_op jit(solution)/shard_map/all_to_all | solution.py:59
  47.8 14.4 %copy-start.3 = (pred[512,1024]{0,1:T(8,128)(4,1)S(1)}, pred[512,1024]{0,1:T(8,128)(4,1)}, u32[]{:S(2)}) copy-start(pred[512,1024]{0,1:T(8,128)(4,1)} %compare_and_fusion) | copy-start | bytes 1572868
  77.7 1.7 copy-start
  98.8 6.5 %copy-start.8 = (s32[1,192]{1,0:T(1,128)S(1)}, s32[1,192]{1,0:T(1,128)}, u32[]{:S(2)}) copy-start(s32[1,192]{1,0:T(1,128)} %param.20) | copy-start | bytes 2308
  98.8 6.4 %copy-start.9 = (s32[1,192]{1,0:T(1,128)S(1)}, s32[1,192]{1,0:T(1,128)}, u32[]{:S(2)}) copy-start(s32[1,192]{1,0:T(1,128)} %param.21) | copy-start | bytes 2308
  100.1 25.9 %all-to-all-start.2 = ((bf16[8,192,512]{2,1,0:T(8,128)(2,1)}), bf16[8,192,512]{2,1,0:T(8,128)(2,1)S(1)}, u32[]{:S(2)}, u32[]{:S(2)}) async-start(bf16[8,192,512]{2,1,0:T(8,128)(2,1)} %bitcast.33), calls=%async_computation.2 | async-start | bytes 3145728 | tf_op jit(solution)/shard_map/all_to_all | solution.py:84
  137.6 47.3 %copy-start.7 = (f32[2048]{0:T(1024)S(1)}, f32[2048]{0:T(1024)}, u32[]{:S(2)}) copy-start(f32[2048]{0:T(1024)} %param.19) | copy-start | bytes 24580
  140.0 40.0 %all-to-all-start.3 = ((bf16[128,1,3,2048]{3,2,1,0:T(4,128)(2,1)}), bf16[128,1,3,2048]{3,2,1,0:T(4,128)(2,1)S(1)}, u32[]{:S(2)}, u32[]{:S(2)}) async-start(bf16[128,1,3,2048]{3,2,1,0:T(4,128)(2,1)} %bitcast.144), calls=%async_computation.3 | async-start | bytes 4194304 | tf_op jit(solution)/shard_map/all_to_all | solution.py:116
  180.0 42.2 %all-to-all-start.5 = ((bf16[128,1,3]{2,1,0:T(2,128)(2,1)}), bf16[128,1,3]{2,1,0:T(2,128)(2,1)S(1)}, u32[]{:S(2)}, u32[]{:S(2)}) async-start(bf16[128,1,3]{2,1,0:T(2,128)(2,1)} %reshape.464), calls=%async_computation.5 | async-start | bytes 131072 | tf_op jit(solution)/shard_map/all_to_all | solution.py:123
  184.9 7.9 %copy-start.11 = (f32[1,1024]{1,0:T(1,128)S(1)}, f32[1,1024]{1,0:T(1,128)}, u32[]{:S(2)}) copy-start(f32[1,1024]{1,0:T(1,128)} %param.17) | copy-start | bytes 12292
  192.8 4.6 %copy-start.10 = (bf16[1,1024,2048]{2,1,0:T(8,128)(2,1)S(1)}, bf16[1,1024,2048]{2,1,0:T(8,128)(2,1)}, u32[]{:S(2)}) copy-start(bf16[1,1024,2048]{2,1,0:T(8,128)(2,1)} %param.18) | copy-start | bytes 12582916
  199.3 1.2 copy-start.1
  222.1 33.8 %all-to-all-start.4 = ((bf16[128,2,3072]{2,1,0:T(2,128)(2,1)}), bf16[128,2,3072]{2,1,0:T(2,128)(2,1)}, u32[]{:S(2)}, u32[]{:S(2)}) async-start(bf16[128,2,3072]{2,1,0:T(2,128)(2,1)} %reshape.472), calls=%async_computation.4 | async-start | bytes 3145728 | tf_op jit(solution)/shard_map/all_to_all | solution.py:149
  269.2 1.2 copy-start.2
Sparse Core Ops, SparseCore 0:
  11.1 89.9 all-gather.1
where the time goes:
time: 284 us; the launch traced here: 280 us
  waiting for transfers between devices  94.6 us (33%)
  local copies, waits for them, and re-layouts  48.2 us (17%)
  matrix products  45.3 us (16%)
  starting transfers between devices  42.1 us (15%)
  other arithmetic  34.8 us (12%)
  between operations  14.7 us (5%)
    all_to_all x1, waiting for transfers between devices, shards(): lax.all_to_all(send_rows.reshape(devices_all, local_experts, capacity, mo...  26.8 us
    unnamed x30, local copies, waits for them, and re-layouts  21.7 us
    all_to_all x1, waiting for transfers between devices, shards(): lax.all_to_all(attended.reshape(seq_groups, local_tokens, heads_here * HE...  20.7 us
    all_to_all x1, waiting for transfers between devices, shards(): lax.all_to_all(query_local, 'seq', split_axis=1, concat_axis=0, tiled=True)  19.7 us
    all_to_all x1, waiting for transfers between devices, shards(): lax.all_to_all(rebuilt.reshape(1, local_experts, slot_total, model_width)...  13.7 us
    all_to_all x1, waiting for transfers between devices, shards(): lax.all_to_all(paired, 'seq', split_axis=1, concat_axis=0, tiled=True)  13 us
    unnamed x2, other arithmetic  12.6 us
    sub x2, other arithmetic, attend_block(): weights = jnp.exp(scores - highest)  12.5 us
  transfers between devices with their start and end apart: 7, of which 5 were waited for; matrix products, arithmetic and copies ran while one was open for 35% of the time, Pallas kernels for 0%

commit v1 on v0

--- a/solution.py
+++ b/solution.py
@@ -3,9 +3,205 @@
 import jax
 import jax.numpy as jnp
 from jax import lax
+from jax.experimental import pallas as pl
+from jax.experimental.pallas import tpu as pltpu
 from jax.sharding import PartitionSpec as P
 
 HEAD_DIMENSION = 128
+MESH = pl.DeviceIdType.MESH
+TILE = 128
+EMPTY = 1e30
+
+
+def widen(src, wide):
+    rows = src.shape[0]
+
+    def step(i, carry):
+        at = pl.ds(pl.multiple_of(i * 384, 384), 384)
+        wide[at, :] = src[at, :].astype(jnp.float32)
+        return carry
+
+    lax.fori_loop(0, rows // 384, step, 0)
+
+
+def narrow(wide, dst):
+    rows = dst.shape[0]
+
+    def step(i, carry):
+        at = pl.ds(pl.multiple_of(i * 384, 384), 384)
+        dst[at, :] = wide[at, :].astype(jnp.bfloat16)
+        return carry
+
+    lax.fori_loop(0, rows // 384, step, 0)
+
+
+def exchange_start(src, dst, send_sem, recv_sem, own_sem, chunk):
+    seq_n, exp_n = lax.axis_size("seq"), lax.axis_size("exp")
+    s, p = lax.axis_index("seq"), lax.axis_index("exp")
+    me = s * exp_n + p
+    mine = pl.ds(pl.multiple_of(me * chunk, chunk), chunk)
+
+    def step(d, carry):
+        to_s = lax.rem(s + d // exp_n, seq_n)
+        to_p = lax.rem(p + lax.rem(d, exp_n), exp_n)
+        other = to_s * exp_n + to_p
+        pltpu.make_async_remote_copy(
+            src_ref=src.at[pl.ds(pl.multiple_of(other * chunk, chunk), chunk)],
+            dst_ref=dst.at[mine],
+            send_sem=send_sem,
+            recv_sem=recv_sem,
+            device_id=(to_s, to_p),
+            device_id_type=MESH,
+        ).start()
+        return carry
+
+    own = pltpu.make_async_copy(src.at[mine], dst.at[mine], own_sem)
+    own.start()
+    lax.fori_loop(1, seq_n * exp_n, step, 0)
+
+
+def exchange_wait(src, dst, send_sem, recv_sem, own_sem, chunk):
+    devices_all = lax.axis_size("seq") * lax.axis_size("exp")
+    pltpu.make_async_copy(src.at[pl.ds(0, chunk)], dst.at[pl.ds(0, chunk)], own_sem).wait()
+    others = pl.ds(0, chunk * (devices_all - 1))
+    pltpu.make_async_copy(src.at[others], dst.at[others], recv_sem).wait()
+    pltpu.make_async_copy(src.at[others], dst.at[others], send_sem).wait()
+
+
+def experts_kernel(
+    h_ref, row_ref, col_ref, encw_hbm, encb_ref, decw_hbm, decb_ref,
+    picked_ref, grad_ref,
+    encw, decw, wide, send, recv, back, ret, slot_rows, centered, latent, gated, residue,
+    weight_sem, own_sem, send_sem, recv_sem,
+):
+    seq_n, exp_n = lax.axis_size("seq"), lax.axis_size("exp")
+    s, p = lax.axis_index("seq"), lax.axis_index("exp")
+    devices_all = seq_n * exp_n
+    tokens, width = h_ref.shape
+    slots = slot_rows.shape[0]
+    latents = latent.shape[1]
+    lanes = width // TILE
+    chunk = slots // devices_all * lanes
+    barrier = pltpu.get_barrier_semaphore()
+
+    def greet(d, carry):
+        to_s = lax.rem(s + d // exp_n, seq_n)
+        to_p = lax.rem(p + lax.rem(d, exp_n), exp_n)
+        pl.semaphore_signal(barrier, inc=1, device_id=(to_s, to_p), device_id_type=MESH)
+        return carry
+
+    lax.fori_loop(1, devices_all, greet, 0)
+    enc_copy = pltpu.make_async_copy(encw_hbm, encw, weight_sem.at[0])
+    dec_copy = pltpu.make_async_copy(decw_hbm, decw, weight_sem.at[1])
+    enc_copy.start()
+    dec_copy.start()
+
+    place = lax.broadcasted_iota(jnp.int32, (slots, tokens), 0) == row_ref[...]
+    pick = jnp.where(place, 1.0, 0.0)
+    free = (1.0 - jnp.sum(pick, axis=1, keepdims=True)) * EMPTY
+    pick = pick.astype(jnp.bfloat16)
+    for n in range(lanes // 2):
+        rows = jnp.dot(
+            pick, h_ref[:, 2 * n * TILE : 2 * (n + 1) * TILE], preferred_element_type=jnp.float32
+        )
+        if n == 0:
+            rows = rows + free
+        wide[pl.ds(2 * n, slots, stride=lanes), :] = rows[:, :TILE]
+        wide[pl.ds(2 * n + 1, slots, stride=lanes), :] = rows[:, TILE:]
+    narrow(wide, send)
+    pl.semaphore_wait(barrier, devices_all - 1)
+    exchange_start(send, recv, send_sem.at[0], recv_sem.at[0], own_sem.at[0], chunk)
+    exchange_wait(send, recv, send_sem.at[0], recv_sem.at[0], own_sem.at[0], chunk)
+
+    widen(recv, wide)
+    live = wide[pl.ds(0, slots, stride=lanes), :][:, :1] < 0.5 * EMPTY
+    for c in range(lanes):
+        at = slice(c * TILE, (c + 1) * TILE)
+        part = wide[pl.ds(c, slots, stride=lanes), :]
+        if c < 2:
+            part = jnp.where(live, part, 0.0)
+        slot_rows[:, at] = part.astype(jnp.bfloat16)
+        centered[:, at] = (part - decb_ref[:, at]).astype(jnp.bfloat16)
+    enc_copy.wait()
+    for n in range(latents // 256):
+        at = slice(n * 256, (n + 1) * 256)
+        pre = jnp.dot(centered[...], encw[:, at], preferred_element_type=jnp.float32)
+        act = jnp.maximum(pre + encb_ref[:, at], 0.0)
+        latent[:, at] = act.astype(jnp.bfloat16)
+        gated[:, at] = jnp.where(live, act, 0.0).astype(jnp.bfloat16)
+    dec_copy.wait()
+    for n in range(lanes // 2):
+        at = slice(2 * n * TILE, 2 * (n + 1) * TILE)
+        rebuilt = jnp.dot(latent[...], decw[:, at], preferred_element_type=jnp.float32)
+        rebuilt = (rebuilt + decb_ref[:, at]).astype(jnp.bfloat16).astype(jnp.float32)
+        residue[:, at] = (rebuilt - slot_rows[:, at].astype(jnp.float32)).astype(jnp.bfloat16)
+        wide[pl.ds(2 * n, slots, stride=lanes), :] = rebuilt[:, :TILE]
+        wide[pl.ds(2 * n + 1, slots, stride=lanes), :] = rebuilt[:, TILE:]
+    narrow(wide, back)
+    exchange_start(back, ret, send_sem.at[1], recv_sem.at[1], own_sem.at[1], chunk)
+
+    def grad_step(n, carry):
+        at = pl.ds(pl.multiple_of(n * 256, 256), 256)
+        grad_ref[at, :] = lax.dot_general(
+            gated[:, at], residue[...], (((0,), (0,)), ((), ())),
+            preferred_element_type=jnp.float32,
+        ).astype(jnp.bfloat16)
+        return carry
+
+    lax.fori_loop(0, latents // 256, grad_step, 0)
+    exchange_wait(back, ret, send_sem.at[1], recv_sem.at[1], own_sem.at[1], chunk)
+
+    widen(ret, wide)
+    for c in range(lanes):
+        slot_rows[:, c * TILE : (c + 1) * TILE] = wide[pl.ds(c, slots, stride=lanes), :].astype(
+            jnp.bfloat16
+        )
+    unplace = lax.broadcasted_iota(jnp.int32, (tokens, slots), 1) == col_ref[...]
+    unpick = jnp.where(unplace, 1.0, 0.0).astype(jnp.bfloat16)
+    for n in range(width // 256):
+        at = slice(n * 256, (n + 1) * 256)
+        picked_ref[:, at] = jnp.dot(
+            unpick, slot_rows[:, at], preferred_element_type=jnp.float32
+        ).astype(jnp.bfloat16)
+
+
+def run_experts(harvested, target, enc_weight, enc_bias, dec_weight, dec_bias, slots):
+    tokens, width = harvested.shape
+    latents = enc_bias.shape[0]
+    lanes = width // TILE
+    vmem = pl.BlockSpec(memory_space=pltpu.VMEM)
+    hbm = pl.BlockSpec(memory_space=pl.ANY)
+    tiles = pltpu.VMEM((slots * lanes, TILE), jnp.bfloat16)
+    return pl.pallas_call(
+        experts_kernel,
+        out_shape=(
+            jax.ShapeDtypeStruct((tokens, width), jnp.bfloat16),
+            jax.ShapeDtypeStruct((latents, width), jnp.bfloat16),
+        ),
+        in_specs=[vmem, vmem, vmem, hbm, vmem, hbm, vmem],
+        out_specs=(vmem, vmem),
+        scratch_shapes=[
+            pltpu.VMEM((width, latents), jnp.bfloat16),
+            pltpu.VMEM((latents, width), jnp.bfloat16),
+            pltpu.VMEM((slots * lanes, TILE), jnp.float32),
+            tiles, tiles, tiles, tiles,
+            pltpu.VMEM((slots, width), jnp.bfloat16),
+            pltpu.VMEM((slots, width), jnp.bfloat16),
+            pltpu.VMEM((slots, latents), jnp.bfloat16),
+            pltpu.VMEM((slots, latents), jnp.bfloat16),
+            pltpu.VMEM((slots, width), jnp.bfloat16),
+            pltpu.SemaphoreType.DMA((2,)),
+            pltpu.SemaphoreType.DMA((2,)),
+            pltpu.SemaphoreType.DMA((2,)),
+            pltpu.SemaphoreType.DMA((2,)),
+        ],
+        compiler_params=pltpu.CompilerParams(
+            collective_id=0, has_side_effects=True, vmem_limit_bytes=48 * 2**20
+        ),
+    )(
+        harvested, target[None, :], target[:, None], enc_weight, enc_bias[None, :], dec_weight,
+        dec_bias[None, :],
+    )
 
 
 masked_score = -1e30
@@ -98,70 +294,21 @@
     local_experts = enc_weight.shape[0]
     experts_all = local_experts * devices_all
     capacity = 2 * local_tokens // experts_all
-    model_width = harvested.shape[1]
     expert_here = expert_ids[0]
     slot_here = slot_ids[0]
     kept_token = slot_here >= 0
     slot_count = experts_all * capacity
     target = jnp.where(kept_token, expert_here * capacity + slot_here, slot_count)
-    send_rows = (
-        jnp.zeros((slot_count, model_width), jnp.bfloat16).at[target].set(harvested, mode="drop")
-    )
-    send_live = (
-        jnp.zeros((slot_count,), jnp.bfloat16)
-        .at[target]
-        .set(jnp.ones((local_tokens,), jnp.bfloat16), mode="drop")
-    )
-    arrived, arrived_live = (
-        lax.all_to_all(
-            send_rows.reshape(devices_all, local_experts, capacity, model_width),
-            ("seq", "exp"),
-            split_axis=0,
-            concat_axis=2,
-            tiled=True,
-        ),
-        lax.all_to_all(
-            send_live.reshape(devices_all, local_experts, capacity),
-            ("seq", "exp"),
-            split_axis=0,
-            concat_axis=2,
-            tiled=True,
-        ),
-    )
-    slot_total = devices_all * capacity
-    slot_rows = arrived.reshape(local_experts, slot_total, model_width)
-    slot_live = arrived_live.reshape(local_experts, slot_total)
-    centered = (slot_rows.astype(jnp.float32) - dec_bias).astype(jnp.bfloat16)
-    pre_act = (
-        jnp.einsum("esd,edf->esf", centered, enc_weight, preferred_element_type=jnp.float32)
-        + enc_bias[:, None, :]
-    )
-    latent = jnp.maximum(pre_act, 0.0).astype(jnp.bfloat16)
-    rebuilt = (
-        jnp.einsum("esf,efd->esd", latent, dec_weight, preferred_element_type=jnp.float32)
-        + dec_bias
-    ).astype(jnp.bfloat16)
-    residue = (rebuilt.astype(jnp.float32) - slot_rows.astype(jnp.float32)).astype(jnp.bfloat16)
-    gated = latent * slot_live[:, :, None]
-    dec_grad = jnp.einsum(
-        "esf,esd->efd", gated, residue, preferred_element_type=jnp.float32
-    ).astype(jnp.bfloat16)
-    returned = lax.all_to_all(
-        rebuilt.reshape(1, local_experts, slot_total, model_width),
-        ("seq", "exp"),
-        split_axis=2,
-        concat_axis=0,
-        tiled=True,
-    )
-    returned = returned.reshape(slot_count, model_width)
-    picked_rows = returned[jnp.minimum(target, slot_count - 1)]
+    picked_rows, dec_grad = run_experts(
+        harvested, target, enc_weight[0], enc_bias[0], dec_weight[0], dec_bias, slot_count
+    )
     reconstruction = jnp.where(
         kept_token[:, None], picked_rows, dec_bias.astype(jnp.bfloat16)[None, :]
     )
     error_rows = (reconstruction.astype(jnp.float32) - harvested.astype(jnp.float32)).astype(
         jnp.bfloat16
     )
-    return (harvested[None], reconstruction[None], error_rows[None], dec_grad)
+    return (harvested[None], reconstruction[None], error_rows[None], dec_grad[None])
 
 
 def solution(mesh):

time: 284 us -> 208 us (0.73); the launches traced: 280 us -> 207 us
  Pallas kernels: 0 us -> 62.2 us
  waiting for transfers between devices: 94.6 us -> 53.9 us
  local copies, waits for them, and re-layouts: 48.2 us -> 9.57 us
  starting transfers between devices: 42.1 us -> 16.4 us
  other arithmetic: 34.8 us -> 19.4 us
  matrix products: 45.3 us -> 31.3 us
    pallas_call x0 -> x1, Pallas kernels: none -> 62.2 us  [run_experts(): pl.pallas_call(experts_kernel, out_shape=(jax.ShapeDtypeStruct((tokens, w...]
    all_to_all x3 -> x0, waiting for transfers between devices: 40.5 us -> none  [the longest x1 26.8 us: shards(): lax.all_to_all(send_rows.reshape(devices_all, local_experts, capacity, mo...]
    all_to_all x3 -> x0, starting transfers between devices: 25.6 us -> none  [the longest x1 10.5 us: shards(): lax.all_to_all(send_rows.reshape(devices_all, local_experts, capacity, mo...]
    unnamed x30 -> x21, local copies, waits for them, and re-layouts: 21.7 us -> 4.35 us
    dot_general x3 -> x0, matrix products: 13.3 us -> none  [the longest x1 6.84 us: shards(): jnp.einsum('esf,esd->efd', gated, residue, preferred_element_type=jnp.flo...]
    unnamed x2 -> x1, other arithmetic: 12.6 us -> 0.02 us
    convert_element_type x2 -> x0, local copies, waits for them, and re-layouts: 8.09 us -> none  [shards(): centered = (slot_rows.astype(jnp.float32) - dec_bias).astype(jnp.bfloat16)]
    reshape x3 -> x0, local copies, waits for them, and re-layouts: 7.29 us -> none  [the longest x1 4.09 us: shards(): rebuilt.reshape(1, local_experts, slot_total, model_width)]
  transfers between devices with their start and end apart: 7 -> 4, of which waited for: 5 -> 3; matrix products, arithmetic and copies ran while one was open for 35% -> 23% of each run, Pallas kernels for 0% -> 0%
where the time goes in v1:
time: 208 us; the launch traced here: 207 us
  Pallas kernels  62.2 us (30%)
  waiting for transfers between devices  53.9 us (26%)
  matrix products  31.3 us (15%)
  other arithmetic  19.4 us (9%)
  starting transfers between devices  16.4 us (8%)
  between operations  14.4 us (7%)
  local copies, waits for them, and re-layouts  9.57 us (5%)
    pallas_call x1, Pallas kernels, run_experts(): pl.pallas_call(experts_kernel, out_shape=(jax.ShapeDtypeStruct((tokens, w...  62.2 us
    all_to_all x1, waiting for transfers between devices, shards(): lax.all_to_all(attended.reshape(seq_groups, local_tokens, heads_here * HE...  20.5 us
    all_to_all x1, waiting for transfers between devices, shards(): lax.all_to_all(query_local, 'seq', split_axis=1, concat_axis=0, tiled=True)  19.7 us
    all_to_all x1, waiting for transfers between devices, shards(): lax.all_to_all(paired, 'seq', split_axis=1, concat_axis=0, tiled=True)  13 us
    sub x2, other arithmetic, attend_block(): weights = jnp.exp(scores - highest)  12.3 us
    dot_general x3, matrix products, attend_block(): jnp.einsum('hqk,kd->qhd', normed, value_part, preferred_element_type=jnp....  11.7 us
    dot_general x1, matrix products, shards(): jnp.dot(head_features, lax.all_gather(out_weight, ('seq', 'exp'), axis=0,...  7.72 us
    sub x1, matrix products, attend_block(): weights = jnp.exp(scores - highest)  7.47 us
  transfers between devices with their start and end apart: 4, of which 3 were waited for; matrix products, arithmetic and copies ran while one was open for 23% of the time, Pallas kernels for 0%

profile of v1, /device:TPU:1, one launch (start us, length us, event | category | flops | bytes accessed | tf_op | source)
XLA Modules:
  0.0 207.1 jit_solution(7645752106242135850)
XLA Ops:
  7.2 0.7 all-gather.2.cloned.1.call-update
  7.9 2.1 %copy.50 = bf16[24,8,8,512]{3,2,1,0:T(8,128)(2,1)S(1)} copy(bf16[24,8,8,512]{3,1,2,0:T(8,128)(2,1)} %bitcast.126) | data formatting | bytes 3145728
  10.0 1.6 copy.23
  11.7 5.8 %all-to-all-start.1 = ((bf16[192,8,512]{2,0,1:T(8,128)(2,1)}), bf16[192,8,512]{2,0,1:T(8,128)(2,1)S(1)}, u32[]{:S(2)}, u32[]{:S(2)}) async-start(bf16[192,8,512]{2,0,1:T(8,128)(2,1)} %copy.23), calls=%async_computation.1 | async-start | bytes 3145728 | tf_op jit(solution)/shard_map/all_to_all | solution.py:254
  18.0 0.3 compare_and_fusion.1
  18.3 1.5 compare_and_fusion
  19.8 19.7 %all-to-all-done.1 = bf16[192,8,512]{2,0,1:T(8,128)(2,1)S(1)} async-done(((bf16[192,8,512]{2,0,1:T(8,128)(2,1)}), bf16[192,8,512]{2,0,1:T(8,128)(2,1)S(1)}, u32[]{:S(2)}, u32[]{:S(2)}) %all-to-all-start.1) | async-done | bytes 1572896 | tf_op jit(solution)/shard_map/all_to_all | solution.py:254
  39.4 0.9 broadcast_in_dim.98
  40.4 5.2 %all-to-all-start = ((bf16[192,8,256]{2,0,1:T(8,128)(2,1)}), bf16[192,8,256]{2,0,1:T(8,128)(2,1)}, u32[]{:S(2)}, u32[]{:S(2)}) async-start(bf16[192,8,256]{2,0,1:T(8,128)(2,1)} %bitcast), calls=%async_computation | async-start | bytes 1572864 | tf_op jit(solution)/shard_map/all_to_all | solution.py:255
  45.5 1.6 fusion.14
  47.1 0.4 reshape.258
  47.5 1.3 fusion.43
  48.9 13.0 %all-to-all-done = bf16[192,8,256]{2,0,1:T(8,128)(2,1)} async-done(((bf16[192,8,256]{2,0,1:T(8,128)(2,1)}), bf16[192,8,256]{2,0,1:T(8,128)(2,1)}, u32[]{:S(2)}, u32[]{:S(2)}) %all-to-all-start) | async-done | bytes 786464 | tf_op jit(solution)/shard_map/all_to_all | solution.py:255
  61.9 7.5 %fusion.46 = (f32[4,512]{1,0:T(4,128)S(1)}, f32[4,512,1024]{1,2,0:T(8,128)}) fusion(pred[512,1024]{0,1:T(8,128)(4,1)} %compare_and_fusion, bf16[512,4,128]{2,1,0:T(4,128)(2,1)S(1)} %get-tuple-element.9, bf16[1536,1,256]{2,0,1:T(8,128)(2,1)} %bitcast.3), kind=kOutput, calls=%fused_computation.70 | convolution fusion | flops 545260544 | bytes 9707520 | tf_op jit(solution)/shard_map/sub | solution.py:217
  69.3 4.2 %fusion.20 = bf16[128,4,512]{2,0,1:T(8,128)(2,1)S(1)} fusion(f32[4,512,1024]{1,2,0:T(8,128)} %get-tuple-element.17, f32[4,512]{1,0:T(4,128)S(1)} %get-tuple-element.16, bf16[1536,1,256]{2,0,1:T(8,128)(2,1)} %bitcast.3), kind=kOutput, calls=%fused_computation.34 | convolution fusion | flops 541327360 | bytes 9183232 | tf_op jit(solution)/shard_map/hqk,kd->qhd/dot_general | solution.py:219
  73.6 0.2 copy.34
  73.8 1.6 fusion.27
  75.4 2.1 %fusion.51 = (f32[4,512]{1,0:T(4,128)S(1)}, f32[4,512,512]{1,2,0:T(8,128)S(1)}) fusion(f32[512,512,4]{1,0,2:T(8,128)S(1)} %fusion.27, pred[512,512]{0,1:T(8,128)(4,1)S(1)} %compare_and_fusion.1), kind=kOutput, calls=%fused_computation.71 | output fusion | flops 6291967 | bytes 8658944 | tf_op jit(solution)/shard_map/sub | solution.py:217
  77.5 1.4 fusion.19
  79.0 0.2 copy.33
  79.2 2.8 %fusion.25 = f32[1536,512,4]{1,0,2:T(8,128)S(1)} fusion(bf16[512,4,128]{2,1,0:T(4,128)(2,1)S(1)} %copy-done.3, bf16[1536,1,256]{2,0,1:T(8,128)(2,1)} %bitcast.3), kind=kOutput, calls=%fused_computation.40 | convolution fusion | flops 805306368 | bytes 13500416 | tf_op jit(solution)/shard_map/qhd,kd->hqk/dot_general | solution.py:212
  82.0 10.2 %fusion.45 = (f32[4,512]{1,0:T(4,128)S(1)}, f32[4,512,1536]{1,2,0:T(8,128)}) fusion(f32[1536,512,4]{1,0,2:T(8,128)S(1)} %fusion.25, pred[512,1536]{0,1:T(8,128)(4,1)} %fusion.14), kind=kOutput, calls=%fused_computation.69 | output fusion | flops 18875904 | bytes 25960448 | tf_op jit(solution)/shard_map/sub | solution.py:217
  92.2 6.1 %fusion.21 = bf16[128,4,512]{2,0,1:T(8,128)(2,1)S(1)} fusion(f32[4,512,1536]{1,2,0:T(8,128)} %get-tuple-element.15, f32[4,512]{1,0:T(4,128)S(1)} %get-tuple-element.14, bf16[1536,1,256]{2,0,1:T(8,128)(2,1)} %bitcast.3), kind=kOutput, calls=%fused_computation.35 | convolution fusion | flops 811859968 | bytes 13508608 | tf_op jit(solution)/shard_map/hqk,kd->qhd/dot_general | solution.py:219
  98.3 0.2 copy.35
  98.5 1.2 pad_maximum_fusion
  99.8 5.4 %all-to-all-start.2 = ((bf16[8,192,512]{2,1,0:T(8,128)(2,1)}), bf16[8,192,512]{2,1,0:T(8,128)(2,1)S(1)}, u32[]{:S(2)}, u32[]{:S(2)}) async-start(bf16[8,192,512]{2,1,0:T(8,128)(2,1)} %bitcast.33), calls=%async_computation.2 | async-start | bytes 3145728 | tf_op jit(solution)/shard_map/all_to_all | solution.py:280
  105.3 20.5 %all-to-all-done.2 = bf16[8,192,512]{2,1,0:T(8,128)(2,1)S(1)} async-done(((bf16[8,192,512]{2,1,0:T(8,128)(2,1)}), bf16[8,192,512]{2,1,0:T(8,128)(2,1)S(1)}, u32[]{:S(2)}, u32[]{:S(2)}) %all-to-all-start.2) | async-done | bytes 1572896 | tf_op jit(solution)/shard_map/all_to_all | solution.py:280
  126.1 7.7 %convolution_convert_fusion.h_ref = bf16[192,2048]{1,0:T(8,128)(2,1)S(1)} fusion(bf16[192,4096]{1,0:T(8,128)(2,1)S(1)} %bitcast.127, bf16[4096,2048]{1,0:T(8,128)(2,1)} %all-gather.2.cloned.1.call-done), kind=kOutput, calls=%fused_computation.25 | convolution fusion | flops 3221618688 | bytes 19136512 | tf_op jit(solution)/shard_map/dot_general | solution.py:288
  133.9 62.2 %shard_map.141 = (bf16[192,2048]{1,0:T(8,128)(2,1)S(1)}, bf16[1024,2048]{1,0:T(8,128)(2,1)S(1)}) custom-call(bf16[192,2048]{1,0:T(8,128)(2,1)S(1)} %convolution_convert_fusion.h_ref, s32[1,192]{1,0:T(1,128)S(1)} %compare_select_fusion.row_ref, s32[192,1]{1,0:T(8,128)S(1)} %copy.37.col_ref, bf16[2048,1024]{1,0:T(8,128)(2,1)} %bitcast.124, ...), custom_call_target="tpu_custom_call" | custom-call | tf_op jit(solution)/shard_map/pallas_call | solution.py:175
  196.1 1.2 fusion.24
  197.3 1.0 fusion.36
  198.3 2.0 copy.70
  (37 shorter events, 0.8 us)
Async XLA Ops:
  7.2 118.9 %all-gather.2.cloned.1.call-start = ((), (), s32[]{:S(2)}) async-start(), calls=%async_computation.3 | async-start | bytes 16908288 | tf_op jit(solution)/shard_map/all_gather | solution.py:290
  7.9 9.6 %copy-start.4 = (bf16[1,192,512]{2,1,0:T(8,128)(2,1)S(1)}, bf16[1,192,512]{2,1,0:T(8,128)(2,1)}, u32[]{:S(2)}) copy-start(bf16[1,192,512]{2,1,0:T(8,128)(2,1)} %param.13) | copy-start | bytes 589828
  7.9 9.6 %copy-start.5 = (bf16[1,192,512]{2,1,0:T(8,128)(2,1)S(1)}, bf16[1,192,512]{2,1,0:T(8,128)(2,1)}, u32[]{:S(2)}) copy-start(bf16[1,192,512]{2,1,0:T(8,128)(2,1)} %param.12) | copy-start | bytes 589828
  10.0 7.9 %copy-start.6 = (s32[1,1536]{1,0:T(1,128)S(1)}, s32[1,1536]{1,0:T(1,128)}, u32[]{:S(2)}) copy-start(s32[1,1536]{1,0:T(1,128)} %param.14) | copy-start | bytes 18436
  10.0 8.2 %slice-start = ((s32[1,1536]{1,0:T(1,128)}), s32[1,1024]{1,0:T(1,128)S(1)}, s32[]{:S(2)}) async-start(s32[1,1536]{1,0:T(1,128)} %param.14), calls=%async_computation.4 | async-start | bytes 8192 | tf_op jit(solution)/shard_map/slice | solution.py:269
  11.7 27.8 %all-to-all-start.1 = ((bf16[192,8,512]{2,0,1:T(8,128)(2,1)}), bf16[192,8,512]{2,0,1:T(8,128)(2,1)S(1)}, u32[]{:S(2)}, u32[]{:S(2)}) async-start(bf16[192,8,512]{2,0,1:T(8,128)(2,1)} %copy.23), calls=%async_computation.1 | async-start | bytes 3145728 | tf_op jit(solution)/shard_map/all_to_all | solution.py:254
  40.4 21.5 %all-to-all-start = ((bf16[192,8,256]{2,0,1:T(8,128)(2,1)}), bf16[192,8,256]{2,0,1:T(8,128)(2,1)}, u32[]{:S(2)}, u32[]{:S(2)}) async-start(bf16[192,8,256]{2,0,1:T(8,128)(2,1)} %bitcast), calls=%async_computation | async-start | bytes 1572864 | tf_op jit(solution)/shard_map/all_to_all | solution.py:255
  77.5 1.7 copy-start.3
  98.3 6.9 %copy-start.7 = (s32[1,192]{1,0:T(1,128)S(1)}, s32[1,192]{1,0:T(1,128)}, u32[]{:S(2)}) copy-start(s32[1,192]{1,0:T(1,128)} %param.20) | copy-start | bytes 2308
  98.3 6.9 %copy-start.8 = (s32[1,192]{1,0:T(1,128)S(1)}, s32[1,192]{1,0:T(1,128)}, u32[]{:S(2)}) copy-start(s32[1,192]{1,0:T(1,128)} %param.21) | copy-start | bytes 2308
  98.3 7.0 %copy-start.1 = (f32[2048]{0:T(1024)S(1)}, f32[2048]{0:T(1024)}, u32[]{:S(2)}) copy-start(f32[2048]{0:T(1024)} %param.19) | copy-start | bytes 24580
  99.8 26.1 %all-to-all-start.2 = ((bf16[8,192,512]{2,1,0:T(8,128)(2,1)}), bf16[8,192,512]{2,1,0:T(8,128)(2,1)S(1)}, u32[]{:S(2)}, u32[]{:S(2)}) async-start(bf16[8,192,512]{2,1,0:T(8,128)(2,1)} %bitcast.33), calls=%async_computation.2 | async-start | bytes 3145728 | tf_op jit(solution)/shard_map/all_to_all | solution.py:280
  126.1 7.8 %copy-start.2 = (f32[1,1024]{1,0:T(1,128)S(1)}, f32[1,1024]{1,0:T(1,128)}, u32[]{:S(2)}) copy-start(f32[1,1024]{1,0:T(1,128)} %encb_ref.1) | copy-start | bytes 12292
  133.9 62.2 %copy-start = (bf16[192,2048]{1,0:T(8,128)(2,1)}, bf16[192,2048]{1,0:T(8,128)(2,1)S(1)}, u32[]{:S(2)}) copy-start(bf16[192,2048]{1,0:T(8,128)(2,1)S(1)} %convolution_convert_fusion.h_ref) | copy-start | bytes 2359300
Sparse Core Ops, SparseCore 0:
  11.1 89.8 all-gather.1

commit v2 on v1

--- a/solution.py
+++ b/solution.py
@@ -11,6 +11,233 @@
 MESH = pl.DeviceIdType.MESH
 TILE = 128
 EMPTY = 1e30
+PARTS = ((0, 384), (384, 256), (640, 384))
+ORDERS = ("xyz", "yzx", "zxy")
+
+
+def attention_kernel(
+    q_ref, k_ref, v_ref, doc_col, doc_row, w_ref,
+    out_ref,
+    kv, w_a, w_b, w_c, attended, bias, result, half_in, send_sem, recv_sem,
+):
+    s, p = lax.axis_index("seq"), lax.axis_index("exp")
+    place = {"x": s // 2, "y": p // 4, "z": lax.rem(p, 4)}
+    core = lax.rem(s, 2)
+    tokens = q_ref.shape[0]
+    kv_width = k_ref.shape[1]
+    span = kv.shape[0] * tokens
+    half = out_ref.shape[1] // 2
+    scale = 1.0 / math.sqrt(HEAD_DIMENSION)
+    parts = (w_a, w_b, w_c)
+    partner = (2 * place["x"] + 1 - core, p)
+
+    def beside(axis, step):
+        at = dict(place)
+        at[axis] = lax.rem(at[axis] + step + 4, 4)
+        return (2 * at["x"] + core, 4 * at["y"] + at["z"])
+
+    peers = [partner] + [beside(axis, step) for axis in "xyz" for step in (1, -1)]
+    barrier = pltpu.get_barrier_semaphore()
+    for peer in peers:
+        pl.semaphore_signal(barrier, inc=1, device_id=peer, device_id_type=MESH)
+
+    started = []
+
+    def send(src, dst, peer):
+        copy = pltpu.make_async_remote_copy(
+            src_ref=src,
+            dst_ref=dst,
+            send_sem=send_sem.at[len(started)],
+            recv_sem=recv_sem.at[len(started)],
+            device_id=peer,
+            device_id_type=MESH,
+        )
+        started.append(copy)
+        copy.start()
+        return copy
+
+    def arrive(copies):
+        for copy in copies:
+            copy.wait_recv()
+
+    kv[s, :, :kv_width] = k_ref[...]
+    kv[s, :, kv_width:] = v_ref[...]
+    for (first, wide), buffer in zip(PARTS, parts):
+        columns = pl.ds(pl.multiple_of(core * half + first, TILE), wide)
+        buffer[place["x"], core, place["y"], place["z"]] = w_ref[:, columns]
+    pl.semaphore_wait(barrier, len(peers))
+
+    kv_near = [send(kv.at[s], kv.at[s], beside("x", step)) for step in (1, -1)]
+    kv_pair = [send(kv.at[s], kv.at[s], partner)]
+    w_pair = []
+    for (first, wide), buffer in zip(PARTS, parts):
+        columns = pl.ds(pl.multiple_of((1 - core) * half + first, TILE), wide)
+        w_pair.append(
+            send(
+                w_ref.at[:, columns],
+                buffer.at[place["x"], core, place["y"], place["z"]],
+                partner,
+            )
+        )
+
+    def block(part, stage, offset, rows):
+        order = ORDERS[part]
+        at = {}
+        for i, axis in enumerate(order):
+            if i < stage:
+                at[axis] = pl.ds(0, 4)
+            elif i == stage:
+                at[axis] = pl.ds(lax.rem(place[axis] + offset + 4, 4), 1)
+            else:
+                at[axis] = pl.ds(place[axis], 1)
+        return parts[part].at[at["x"], rows, at["y"], at["z"]]
+
+    def stage_near(stage):
+        copies = []
+        for part in range(3):
+            axis = ORDERS[part][stage]
+            for step in (1, -1):
+                view = block(part, stage, 0, pl.ds(0, 2))
+                copies.append(send(view, view, beside(axis, step)))
+        return copies
+
+    def stage_far(stage):
+        copies = []
+        for part in range(3):
+            axis = ORDERS[part][stage]
+            for step, row in ((1, 0), (-1, 1)):
+                view = block(part, stage, -step, pl.ds(row, 1))
+                copies.append(send(view, view, beside(axis, step)))
+        return copies
+
+    def kv_far():
+        copies, pair = [], []
+        for step, first in ((1, 0), (-1, tokens // 2)):
+            origin = 2 * lax.rem(place["x"] - step + 4, 4) + core
+            view = kv.at[origin, pl.ds(first, tokens // 2)]
+            copies.append(send(view, view, beside("x", step)))
+        for step in (1, -1):
+            view = kv.at[2 * lax.rem(place["x"] - step + 4, 4) + core]
+            pair.append(send(view, view, partner))
+        return copies, pair
+
+    arrive(w_pair)
+    near = stage_near(0)
+    rows_at = s * tokens + lax.broadcasted_iota(jnp.int32, (tokens, span), 0)
+    keys_at = lax.broadcasted_iota(jnp.int32, (tokens, span), 1)
+    visible = (rows_at >= keys_at) & (doc_col[...] == doc_row[...])
+    bias[...] = jnp.where(visible, 0.0, -EMPTY)
+    arrive(near)
+    far = stage_far(0)
+    arrive(far)
+    near = stage_near(1)
+    arrive(kv_near)
+    kv_across, pair = kv_far()
+    kv_pair += pair
+    arrive(near)
+    far = stage_far(1)
+    arrive(far)
+    near = stage_near(2)
+    arrive(kv_across)
+    view = kv.at[2 * lax.rem(place["x"] + 2, 4) + core]
+    kv_pair.append(send(view, view, partner))
+    arrive(kv_pair)
+
+    heads = q_ref.shape[1] // HEAD_DIMENSION
+    group = heads // (kv_width // HEAD_DIMENSION)
+
+    def attend(first, last, blocks):
+        keys = blocks * tokens
+
+        def one_head(h, carry):
+            g = h // group
+            q_at = pl.ds(pl.multiple_of(h * HEAD_DIMENSION, HEAD_DIMENSION), HEAD_DIMENSION)
+            k_at = pl.ds(pl.multiple_of(g * HEAD_DIMENSION, HEAD_DIMENSION), HEAD_DIMENSION)
+            v_at = pl.ds(
+                pl.multiple_of(kv_width + g * HEAD_DIMENSION, HEAD_DIMENSION), HEAD_DIMENSION
+            )
+            key_part = kv[:blocks, :, k_at].reshape(keys, HEAD_DIMENSION)
+            value_part = kv[:blocks, :, v_at].reshape(keys, HEAD_DIMENSION)
+            scores = lax.dot_general(
+                q_ref[:, q_at], key_part, (((1,), (1,)), ((), ())),
+                preferred_element_type=jnp.float32,
+            )
+            scores = scores + bias[:, :keys]
+            highest = jnp.max(scores, axis=1, keepdims=True)
+            weights = jnp.exp2((scores - highest) * (scale * math.log2(math.e)))
+            total = jnp.sum(weights, axis=1, keepdims=True)
+            mixed = jnp.dot(
+                weights.astype(jnp.bfloat16), value_part, preferred_element_type=jnp.float32
+            )
+            attended[core, :, q_at] = (mixed / total).astype(jnp.bfloat16)
+            return carry
+
+        lax.fori_loop(first, last, one_head, 0)
+
+    def attend_heads(first, last):
+        for chips in range(1, 5):
+
+            @pl.when(place["x"] == chips - 1)
+            def _():
+                attend(first, last, 2 * chips)
+
+        columns = pl.ds(first * HEAD_DIMENSION, (last - first) * HEAD_DIMENSION)
+        view = attended.at[core, :, columns]
+        return send(view, view, partner)
+
+    across = [attend_heads(0, heads // 2)]
+    arrive(near)
+    far = stage_far(2)
+    across.append(attend_heads(heads // 2, heads))
+    arrive(far)
+    arrive(across)
+
+    rows = attended.shape[1] * 2
+    for (first, wide), buffer in zip(PARTS, parts):
+        for n in range(0, wide, TILE):
+            weight = buffer[:, :, :, :, :, n : n + TILE].reshape(heads * HEAD_DIMENSION, TILE)
+            both = jnp.dot(
+                attended[...].reshape(rows, heads * HEAD_DIMENSION),
+                weight,
+                preferred_element_type=jnp.float32,
+            )
+            result[:, :, first + n : first + n + TILE] = both.astype(jnp.bfloat16).reshape(
+                2, tokens, TILE
+            )
+    back = send(result.at[1 - core], half_in, partner)
+    out_ref[:, pl.ds(pl.multiple_of(core * half, half), half)] = result[core]
+    arrive([back])
+    out_ref[:, pl.ds(pl.multiple_of((1 - core) * half, half), half)] = half_in[...]
+    for copy in started:
+        copy.wait_send()
+
+
+def run_attention(query, key, value, doc_mine, doc_all, out_weight, seq_groups):
+    tokens, q_width = query.shape
+    kv_width = key.shape[1]
+    span = tokens * seq_groups
+    rows, width = out_weight.shape
+    vmem = pl.BlockSpec(memory_space=pltpu.VMEM)
+    copies = 64
+    return pl.pallas_call(
+        attention_kernel,
+        out_shape=jax.ShapeDtypeStruct((tokens, width), jnp.bfloat16),
+        in_specs=[vmem] * 6,
+        out_specs=vmem,
+        scratch_shapes=[
+            pltpu.VMEM((seq_groups, tokens, 2 * kv_width), jnp.bfloat16),
+            *[pltpu.VMEM((4, 2, 4, 4, rows, wide), jnp.bfloat16) for _, wide in PARTS],
+            pltpu.VMEM((2, tokens, q_width), jnp.bfloat16),
+            pltpu.VMEM((tokens, span), jnp.float32),
+            pltpu.VMEM((2, tokens, width // 2), jnp.bfloat16),
+            pltpu.VMEM((tokens, width // 2), jnp.bfloat16),
+            pltpu.SemaphoreType.DMA((copies,)),
+            pltpu.SemaphoreType.DMA((copies,)),
+        ],
+        compiler_params=pltpu.CompilerParams(
+            collective_id=1, has_side_effects=True, vmem_limit_bytes=48 * 2**20
+        ),
+    )(query, key, value, doc_mine[:, None], doc_all[None, :], out_weight)
 
 
 def widen(src, wide):
@@ -204,22 +431,6 @@
     )
 
 
-masked_score = -1e30
-
-
-def attend_block(query_block, key_part, value_part, visible, score_scale):
-    scores = (
-        jnp.einsum("qhd,kd->hqk", query_block, key_part, preferred_element_type=jnp.float32)
-        * score_scale
-    )
-    scores = jnp.where(visible[None, :, :], scores, masked_score)
-    highest = jnp.max(scores, axis=2, keepdims=True)
-    weights = jnp.exp(scores - highest)
-    normed = (weights / jnp.sum(weights, axis=2, keepdims=True)).astype(jnp.bfloat16)
-    mixed = jnp.einsum("hqk,kd->qhd", normed, value_part, preferred_element_type=jnp.float32)
-    return mixed.astype(jnp.bfloat16)
-
-
 def shards(
     query_rows,
     key_rows,
@@ -237,60 +448,13 @@
     seq_groups = lax.axis_size("seq")
     exp_groups = lax.axis_size("exp")
     devices_all = seq_groups * exp_groups
-    query_heads = query_rows.shape[2] // HEAD_DIMENSION
-    kv_heads = key_rows.shape[2] // HEAD_DIMENSION
-    heads_here = query_heads // seq_groups
-    kv_share = seq_groups // kv_heads
-    query_local = query_rows[0].reshape(local_tokens, seq_groups, heads_here * HEAD_DIMENSION)
-    paired = jnp.concatenate(
-        [
-            key_rows[0].reshape(local_tokens, kv_heads, HEAD_DIMENSION),
-            value_matrix[0].reshape(local_tokens, kv_heads, HEAD_DIMENSION),
-        ],
-        axis=2,
-    )
-    paired = jnp.repeat(paired, kv_share, axis=1)
-    query_all, paired_all = (
-        lax.all_to_all(query_local, "seq", split_axis=1, concat_axis=0, tiled=True),
-        lax.all_to_all(paired, "seq", split_axis=1, concat_axis=0, tiled=True),
-    )
-    span_length = local_tokens * seq_groups
-    query_all = query_all.reshape(span_length, heads_here, HEAD_DIMENSION)
-    key_all = paired_all[:, 0, :HEAD_DIMENSION]
-    value_all = paired_all[:, 0, HEAD_DIMENSION:]
     doc_row = doc_ids[0]
-    positions = jnp.arange(span_length)
-    block_rows = 512
-    score_scale = 1.0 / math.sqrt(HEAD_DIMENSION)
-    pieces_out = []
-    for row_start in range(0, span_length, block_rows):
-        row_stop = row_start + block_rows
-        visible = (positions[row_start:row_stop, None] >= positions[None, :row_stop]) & (
-            doc_row[row_start:row_stop, None] == doc_row[None, :row_stop]
-        )
-        mixed = attend_block(
-            query_all[row_start:row_stop],
-            key_all[:row_stop],
-            value_all[:row_stop],
-            visible,
-            score_scale,
-        )
-        pieces_out.append(mixed.reshape(block_rows, heads_here * HEAD_DIMENSION))
-    attended = jnp.concatenate(pieces_out, axis=0)
-    heads_back = lax.all_to_all(
-        attended.reshape(seq_groups, local_tokens, heads_here * HEAD_DIMENSION),
-        "seq",
-        split_axis=0,
-        concat_axis=2,
-        tiled=True,
-    )
-    head_features = heads_back[0]
-    projected = jnp.dot(
-        head_features,
-        lax.all_gather(out_weight, ("seq", "exp"), axis=0, tiled=True),
-        preferred_element_type=jnp.float32,
-    )
-    harvested = projected.astype(jnp.bfloat16)
+    doc_mine = lax.dynamic_slice_in_dim(
+        doc_row, lax.axis_index("seq") * local_tokens, local_tokens
+    )
+    harvested = run_attention(
+        query_rows[0], key_rows[0], value_matrix[0], doc_mine, doc_row, out_weight, seq_groups
+    )
     local_experts = enc_weight.shape[0]
     experts_all = local_experts * devices_all
     capacity = 2 * local_tokens // experts_all

time: 208 us -> 146 us (0.70)
  Pallas kernels: 62.2 us -> 132 us
  waiting for transfers between devices: 53.9 us -> 0 us
  matrix products: 31.3 us -> 0 us
  other arithmetic: 19.4 us -> 2.91 us
  starting transfers between devices: 16.4 us -> 0 us
  between operations: 14.4 us -> 0.71 us
    pallas_call x0 -> x1, Pallas kernels: none -> 71.5 us  [run_attention(): pl.pallas_call(attention_kernel, out_shape=jax.ShapeDtypeStruct((tokens,...]
    all_to_all x3 -> x0, waiting for transfers between devices: 53.2 us -> none  [the longest x1 20.5 us: shards(): lax.all_to_all(attended.reshape(seq_groups, local_tokens, heads_here * HE...]
    dot_general x6 -> x0, matrix products: 23.9 us -> none  [the longest x3 11.7 us: attend_block(): jnp.einsum('hqk,kd->qhd', normed, value_part, preferred_element_type=jnp....]
    all_to_all x3 -> x0, starting transfers between devices: 16.3 us -> none  [the longest x1 5.8 us: shards(): lax.all_to_all(query_local, 'seq', split_axis=1, concat_axis=0, tiled=True)]
    sub x2 -> x0, other arithmetic: 12.3 us -> none  [attend_block(): weights = jnp.exp(scores - highest)]
    sub x1 -> x0, matrix products: 7.47 us -> none  [attend_block(): weights = jnp.exp(scores - highest)]
    unnamed x21 -> x18, local copies, waits for them, and re-layouts: 4.35 us -> 9.13 us
    and x3 -> x0, other arithmetic: 3.38 us -> none  [shards(): (positions[row_start:row_stop, None] >= positions[None, :row_stop]) & (do...]
  transfers between devices with their start and end apart: 4 -> 0, of which waited for: 3 -> 0; matrix products, arithmetic and copies ran while one was open for 23% -> 0% of each run, Pallas kernels for 0% -> 0%
where the time goes in v2:
time: 146 us
  Pallas kernels  132 us (90%)
  local copies, waits for them, and re-layouts  10.1 us (7%)
  other arithmetic  2.91 us (2%)
    pallas_call x1, Pallas kernels, run_attention(): pl.pallas_call(attention_kernel, out_shape=jax.ShapeDtypeStruct((tokens,...  71.5 us
    pallas_call x1, Pallas kernels, run_experts(): pl.pallas_call(experts_kernel, out_shape=(jax.ShapeDtypeStruct((tokens, w...  60.8 us
    unnamed x18, local copies, waits for them, and re-layouts  9.13 us

profile of v2, /device:TPU:1, one launch (start us, length us, event | category | flops | bytes accessed | tf_op | source)
XLA Modules:
  0.0 146.0 jit_solution(1728340320876573026)
XLA Ops:
  0.6 0.8 dynamic-slice_bitcast_fusion
  1.4 0.1 copy.15.doc_col
  1.5 0.0 copy-start
  1.5 1.4 copy-done
  2.9 0.0 copy-start.1
  2.9 0.9 copy-done.1
  3.9 0.0 copy-start.2
  3.9 0.9 copy-done.2
  4.8 0.0 copy-start.3
  4.8 0.9 copy-done.3
  5.7 0.0 copy-start.5
  5.7 0.7 copy-done.5
  6.4 71.5 %shard_map.138.h_ref = bf16[192,2048]{1,0:T(8,128)(2,1)S(1)} custom-call(bf16[192,4096]{1,0:T(8,128)(2,1)S(1)} %bitcast.17, bf16[192,512]{1,0:T(8,128)(2,1)S(1)} %bitcast.18, bf16[192,512]{1,0:T(8,128)(2,1)S(1)} %bitcast.19, s32[192,1]{1,0:T(8,128)S(1)} %copy.15.doc_col, s32[1,1536]{1,0:T(1,128)S(1)} %copy-done.5, bf16[32,2048]{1,0:T(8,128)(2,1)S(1)} %copy-done.3), custom_call_target="tpu_custom_call" | custom-call | tf_op jit(solution)/shard_map/pallas_call | solution.py:222
  77.9 0.7 compare_select_fusion.row_ref
  78.6 0.1 copy.16.col_ref
  78.7 0.0 copy-start.4
  78.7 0.7 copy-done.4
  79.4 0.0 copy-start.6
  79.4 0.7 copy-done.6
  80.1 0.0 copy-start.7
  80.1 60.8 %shard_map.139 = (bf16[192,2048]{1,0:T(8,128)(2,1)S(1)}, bf16[1024,2048]{1,0:T(8,128)(2,1)S(1)}) custom-call(bf16[192,2048]{1,0:T(8,128)(2,1)S(1)} %shard_map.138.h_ref, s32[1,192]{1,0:T(1,128)S(1)} %compare_select_fusion.row_ref, s32[192,1]{1,0:T(8,128)S(1)} %copy.16.col_ref, bf16[2048,1024]{1,0:T(8,128)(2,1)} %bitcast.22, f32[1,1024]{1,0:T(1,128)S(1)} %copy-done.6, ...), custom_call_target="tpu_custom_call" | custom-call | tf_op jit(solution)/shard_map/pallas_call | solution.py:402
  140.9 0.0 copy-done.7
  140.9 1.2 fusion
  142.1 1.0 fusion.1
  143.1 0.9 copy.19
  144.0 2.0 %copy.20 = bf16[1,1024,2048]{2,1,0:T(8,128)(2,1)} copy(bf16[1,1024,2048]{2,1,0:T(8,128)(2,1)S(1)} %bitcast.16) | data formatting | bytes 8388608
  (2 shorter events, 0.0 us)
Async XLA Ops:
  1.5 1.4 copy-start
  2.9 0.9 copy-start.1
  3.9 0.9 copy-start.2
  4.8 0.9 copy-start.3
  5.7 0.7 copy-start.5
  78.7 0.7 copy-start.4
  79.4 0.7 copy-start.6
  80.1 60.8 %copy-start.7 = (s32[1,192]{1,0:T(1,128)S(1)}, s32[1,192]{1,0:T(1,128)}, u32[]{:S(2)}) copy-start(s32[1,192]{1,0:T(1,128)} %param.21) | copy-start | bytes 2308

commit v3 on v2

--- a/solution.py
+++ b/solution.py
@@ -240,132 +240,169 @@
     )(query, key, value, doc_mine[:, None], doc_all[None, :], out_weight)
 
 
-def widen(src, wide):
-    rows = src.shape[0]
-
+GROUPS = 4
+
+
+def widen(src, wide, first, rows):
     def step(i, carry):
-        at = pl.ds(pl.multiple_of(i * 384, 384), 384)
+        at = pl.ds(pl.multiple_of(first + i * 384, 384), 384)
         wide[at, :] = src[at, :].astype(jnp.float32)
         return carry
 
     lax.fori_loop(0, rows // 384, step, 0)
 
 
-def narrow(wide, dst):
-    rows = dst.shape[0]
-
+def narrow(wide, dst, first, rows):
     def step(i, carry):
-        at = pl.ds(pl.multiple_of(i * 384, 384), 384)
+        at = pl.ds(pl.multiple_of(first + i * 384, 384), 384)
         dst[at, :] = wide[at, :].astype(jnp.bfloat16)
         return carry
 
     lax.fori_loop(0, rows // 384, step, 0)
 
 
-def exchange_start(src, dst, send_sem, recv_sem, own_sem, chunk):
-    seq_n, exp_n = lax.axis_size("seq"), lax.axis_size("exp")
+def peer_at(group, i, sign):
     s, p = lax.axis_index("seq"), lax.axis_index("exp")
-    me = s * exp_n + p
-    mine = pl.ds(pl.multiple_of(me * chunk, chunk), chunk)
-
-    def step(d, carry):
-        to_s = lax.rem(s + d // exp_n, seq_n)
-        to_p = lax.rem(p + lax.rem(d, exp_n), exp_n)
-        other = to_s * exp_n + to_p
+    along_x, along_y, across = i // 8, lax.rem(i // 2, 4), lax.rem(i, 2)
+    along_z = lax.rem(group + 8 - along_x - along_y, 4)
+    x = lax.rem(s // 2 + sign * along_x + 4, 4)
+    y = lax.rem(p // 4 + sign * along_y + 4, 4)
+    z = lax.rem(lax.rem(p, 4) + sign * along_z + 4, 4)
+    return (2 * x + lax.rem(s + across, 2), 4 * y + z)
+
+
+def place_of(expert):
+    s, p = lax.axis_index("seq"), lax.axis_index("exp")
+    to_s, to_p = expert // 16, expert % 16
+    along_x = (to_s // 2 - s // 2 + 4) % 4
+    along_y = (to_p // 4 - p // 4 + 4) % 4
+    along_z = (to_p % 4 - p % 4 + 4) % 4
+    across = (to_s + s) % 2
+    return (along_x + along_y + along_z) % 4 * 32 + along_x * 8 + along_y * 2 + across
+
+
+def exchange_start(group, sign, src, dst, send_sem, recv_sem, own_sem, chunk):
+    members = src.shape[0] // chunk // GROUPS
+
+    def step(i, carry):
+        at = pl.ds(pl.multiple_of((group * members + i) * chunk, chunk), chunk)
         pltpu.make_async_remote_copy(
-            src_ref=src.at[pl.ds(pl.multiple_of(other * chunk, chunk), chunk)],
-            dst_ref=dst.at[mine],
-            send_sem=send_sem,
-            recv_sem=recv_sem,
-            device_id=(to_s, to_p),
+            src_ref=src.at[at],
+            dst_ref=dst.at[at],
+            send_sem=send_sem.at[group],
+            recv_sem=recv_sem.at[group],
+            device_id=peer_at(group, i, sign),
             device_id_type=MESH,
         ).start()
         return carry
 
-    own = pltpu.make_async_copy(src.at[mine], dst.at[mine], own_sem)
-    own.start()
-    lax.fori_loop(1, seq_n * exp_n, step, 0)
-
-
-def exchange_wait(src, dst, send_sem, recv_sem, own_sem, chunk):
-    devices_all = lax.axis_size("seq") * lax.axis_size("exp")
-    pltpu.make_async_copy(src.at[pl.ds(0, chunk)], dst.at[pl.ds(0, chunk)], own_sem).wait()
-    others = pl.ds(0, chunk * (devices_all - 1))
-    pltpu.make_async_copy(src.at[others], dst.at[others], recv_sem).wait()
-    pltpu.make_async_copy(src.at[others], dst.at[others], send_sem).wait()
+    if group == 0:
+        own = pl.ds(0, chunk)
+        pltpu.make_async_copy(src.at[own], dst.at[own], own_sem).start()
+    lax.fori_loop(1 if group == 0 else 0, members, step, 0)
+
+
+def group_rows(group, src, chunk):
+    members = src.shape[0] // chunk // GROUPS
+    first = group * members + (1 if group == 0 else 0)
+    return pl.ds(first * chunk, ((group + 1) * members - first) * chunk)
+
+
+def exchange_wait(group, src, dst, recv_sem, own_sem, chunk):
+    if group == 0:
+        own = pl.ds(0, chunk)
+        pltpu.make_async_copy(src.at[own], dst.at[own], own_sem).wait()
+    at = group_rows(group, src, chunk)
+    pltpu.make_async_copy(src.at[at], dst.at[at], recv_sem.at[group]).wait()
+
+
+def exchange_sent(group, src, dst, send_sem, chunk):
+    at = group_rows(group, src, chunk)
+    pltpu.make_async_copy(src.at[at], dst.at[at], send_sem.at[group]).wait()
 
 
 def experts_kernel(
     h_ref, row_ref, col_ref, encw_hbm, encb_ref, decw_hbm, decb_ref,
     picked_ref, grad_ref,
     encw, decw, wide, send, recv, back, ret, slot_rows, centered, latent, gated, residue,
-    weight_sem, own_sem, send_sem, recv_sem,
+    weight_sem, own_sem, send_sem, recv_sem, send_back_sem, recv_back_sem,
 ):
-    seq_n, exp_n = lax.axis_size("seq"), lax.axis_size("exp")
-    s, p = lax.axis_index("seq"), lax.axis_index("exp")
-    devices_all = seq_n * exp_n
     tokens, width = h_ref.shape
     slots = slot_rows.shape[0]
     latents = latent.shape[1]
     lanes = width // TILE
-    chunk = slots // devices_all * lanes
+    members = lax.axis_size("seq") * lax.axis_size("exp") // GROUPS
+    chunk = slots // (members * GROUPS) * lanes
+    part_slots = slots // GROUPS
+    part_rows = part_slots * lanes
     barrier = pltpu.get_barrier_semaphore()
 
-    def greet(d, carry):
-        to_s = lax.rem(s + d // exp_n, seq_n)
-        to_p = lax.rem(p + lax.rem(d, exp_n), exp_n)
-        pl.semaphore_signal(barrier, inc=1, device_id=(to_s, to_p), device_id_type=MESH)
-        return carry
-
-    lax.fori_loop(1, devices_all, greet, 0)
+    for group in range(GROUPS):
+
+        def greet(i, carry):
+            pl.semaphore_signal(
+                barrier, inc=1, device_id=peer_at(group, i, 1), device_id_type=MESH
+            )
+            return carry
+
+        lax.fori_loop(1 if group == 0 else 0, members, greet, 0)
     enc_copy = pltpu.make_async_copy(encw_hbm, encw, weight_sem.at[0])
     dec_copy = pltpu.make_async_copy(decw_hbm, decw, weight_sem.at[1])
     enc_copy.start()
     dec_copy.start()
 
-    place = lax.broadcasted_iota(jnp.int32, (slots, tokens), 0) == row_ref[...]
-    pick = jnp.where(place, 1.0, 0.0)
-    free = (1.0 - jnp.sum(pick, axis=1, keepdims=True)) * EMPTY
-    pick = pick.astype(jnp.bfloat16)
-    for n in range(lanes // 2):
-        rows = jnp.dot(
-            pick, h_ref[:, 2 * n * TILE : 2 * (n + 1) * TILE], preferred_element_type=jnp.float32
-        )
-        if n == 0:
-            rows = rows + free
-        wide[pl.ds(2 * n, slots, stride=lanes), :] = rows[:, :TILE]
-        wide[pl.ds(2 * n + 1, slots, stride=lanes), :] = rows[:, TILE:]
-    narrow(wide, send)
-    pl.semaphore_wait(barrier, devices_all - 1)
-    exchange_start(send, recv, send_sem.at[0], recv_sem.at[0], own_sem.at[0], chunk)
-    exchange_wait(send, recv, send_sem.at[0], recv_sem.at[0], own_sem.at[0], chunk)
-
-    widen(recv, wide)
-    live = wide[pl.ds(0, slots, stride=lanes), :][:, :1] < 0.5 * EMPTY
-    for c in range(lanes):
-        at = slice(c * TILE, (c + 1) * TILE)
-        part = wide[pl.ds(c, slots, stride=lanes), :]
-        if c < 2:
-            part = jnp.where(live, part, 0.0)
-        slot_rows[:, at] = part.astype(jnp.bfloat16)
-        centered[:, at] = (part - decb_ref[:, at]).astype(jnp.bfloat16)
+    for group in range(GROUPS):
+        first = group * part_rows
+        place = lax.broadcasted_iota(jnp.int32, (part_slots, tokens), 0) + group * part_slots
+        pick = jnp.where(place == row_ref[...], 1.0, 0.0)
+        free = (1.0 - jnp.sum(pick, axis=1, keepdims=True)) * EMPTY
+        pick = pick.astype(jnp.bfloat16)
+        for n in range(lanes // 2):
+            rows = jnp.dot(
+                pick,
+                h_ref[:, 2 * n * TILE : 2 * (n + 1) * TILE],
+                preferred_element_type=jnp.float32,
+            )
+            if n == 0:
+                rows = rows + free
+            wide[pl.ds(first + 2 * n, part_slots, stride=lanes), :] = rows[:, :TILE]
+            wide[pl.ds(first + 2 * n + 1, part_slots, stride=lanes), :] = rows[:, TILE:]
+        narrow(wide, send, first, part_rows)
+        if group == 0:
+            pl.semaphore_wait(barrier, members * GROUPS - 1)
+        exchange_start(group, 1, send, recv, send_sem, recv_sem, own_sem.at[0], chunk)
+
     enc_copy.wait()
-    for n in range(latents // 256):
-        at = slice(n * 256, (n + 1) * 256)
-        pre = jnp.dot(centered[...], encw[:, at], preferred_element_type=jnp.float32)
-        act = jnp.maximum(pre + encb_ref[:, at], 0.0)
-        latent[:, at] = act.astype(jnp.bfloat16)
-        gated[:, at] = jnp.where(live, act, 0.0).astype(jnp.bfloat16)
     dec_copy.wait()
-    for n in range(lanes // 2):
-        at = slice(2 * n * TILE, 2 * (n + 1) * TILE)
-        rebuilt = jnp.dot(latent[...], decw[:, at], preferred_element_type=jnp.float32)
-        rebuilt = (rebuilt + decb_ref[:, at]).astype(jnp.bfloat16).astype(jnp.float32)
-        residue[:, at] = (rebuilt - slot_rows[:, at].astype(jnp.float32)).astype(jnp.bfloat16)
-        wide[pl.ds(2 * n, slots, stride=lanes), :] = rebuilt[:, :TILE]
-        wide[pl.ds(2 * n + 1, slots, stride=lanes), :] = rebuilt[:, TILE:]
-    narrow(wide, back)
-    exchange_start(back, ret, send_sem.at[1], recv_sem.at[1], own_sem.at[1], chunk)
+    for group in range(GROUPS):
+        first = group * part_rows
+        mine = slice(group * part_slots, (group + 1) * part_slots)
+        exchange_wait(group, send, recv, recv_sem, own_sem.at[0], chunk)
+        widen(recv, wide, first, part_rows)
+        live = wide[pl.ds(first, part_slots, stride=lanes), :][:, :1] < 0.5 * EMPTY
+        for c in range(lanes):
+            at = slice(c * TILE, (c + 1) * TILE)
+            part = wide[pl.ds(first + c, part_slots, stride=lanes), :]
+            if c < 2:
+                part = jnp.where(live, part, 0.0)
+            slot_rows[mine, at] = part.astype(jnp.bfloat16)
+            centered[mine, at] = (part - decb_ref[:, at]).astype(jnp.bfloat16)
+        for n in range(latents // 256):
+            at = slice(n * 256, (n + 1) * 256)
+            pre = jnp.dot(centered[mine, :], encw[:, at], preferred_element_type=jnp.float32)
+            act = jnp.maximum(pre + encb_ref[:, at], 0.0)
+            latent[mine, at] = act.astype(jnp.bfloat16)
+            gated[mine, at] = jnp.where(live, act, 0.0).astype(jnp.bfloat16)
+        for n in range(lanes // 2):
+            at = slice(2 * n * TILE, 2 * (n + 1) * TILE)
+            rebuilt = jnp.dot(latent[mine, :], decw[:, at], preferred_element_type=jnp.float32)
+            rebuilt = (rebuilt + decb_ref[:, at]).astype(jnp.bfloat16).astype(jnp.float32)
+            error = rebuilt - slot_rows[mine, at].astype(jnp.float32)
+            residue[mine, at] = error.astype(jnp.bfloat16)
+            wide[pl.ds(first + 2 * n, part_slots, stride=lanes), :] = rebuilt[:, :TILE]
+            wide[pl.ds(first + 2 * n + 1, part_slots, stride=lanes), :] = rebuilt[:, TILE:]
+        narrow(wide, back, first, part_rows)
+        exchange_start(group, -1, back, ret, send_back_sem, recv_back_sem, own_sem.at[1], chunk)
 
     def grad_step(n, carry):
         at = pl.ds(pl.multiple_of(n * 256, 256), 256)
@@ -376,20 +413,26 @@
         return carry
 
     lax.fori_loop(0, latents // 256, grad_step, 0)
-    exchange_wait(back, ret, send_sem.at[1], recv_sem.at[1], own_sem.at[1], chunk)
-
-    widen(ret, wide)
-    for c in range(lanes):
-        slot_rows[:, c * TILE : (c + 1) * TILE] = wide[pl.ds(c, slots, stride=lanes), :].astype(
-            jnp.bfloat16
-        )
     unplace = lax.broadcasted_iota(jnp.int32, (tokens, slots), 1) == col_ref[...]
     unpick = jnp.where(unplace, 1.0, 0.0).astype(jnp.bfloat16)
+
+    for group in range(GROUPS):
+        first = group * part_rows
+        mine = slice(group * part_slots, (group + 1) * part_slots)
+        exchange_wait(group, back, ret, recv_back_sem, own_sem.at[1], chunk)
+        widen(ret, wide, first, part_rows)
+        for c in range(lanes):
+            slot_rows[mine, c * TILE : (c + 1) * TILE] = wide[
+                pl.ds(first + c, part_slots, stride=lanes), :
+            ].astype(jnp.bfloat16)
     for n in range(width // 256):
         at = slice(n * 256, (n + 1) * 256)
         picked_ref[:, at] = jnp.dot(
             unpick, slot_rows[:, at], preferred_element_type=jnp.float32
         ).astype(jnp.bfloat16)
+    for group in range(GROUPS):
+        exchange_sent(group, send, recv, send_sem, chunk)
+        exchange_sent(group, back, ret, send_back_sem, chunk)
 
 
 def run_experts(harvested, target, enc_weight, enc_bias, dec_weight, dec_bias, slots):
@@ -419,8 +462,7 @@
             pltpu.VMEM((slots, width), jnp.bfloat16),
             pltpu.SemaphoreType.DMA((2,)),
             pltpu.SemaphoreType.DMA((2,)),
-            pltpu.SemaphoreType.DMA((2,)),
-            pltpu.SemaphoreType.DMA((2,)),
+            *[pltpu.SemaphoreType.DMA((GROUPS,))] * 4,
         ],
         compiler_params=pltpu.CompilerParams(
             collective_id=0, has_side_effects=True, vmem_limit_bytes=48 * 2**20
@@ -429,6 +471,42 @@
         harvested, target[None, :], target[:, None], enc_weight, enc_bias[None, :], dec_weight,
         dec_bias[None, :],
     )
+
+
+def finish_kernel(h_ref, picked_ref, kept_ref, bias_ref, grad_ref,
+                  h_out, recon_out, error_out, grad_out, recon, error, sem):
+    grad_copy = pltpu.make_async_copy(grad_ref, grad_out, sem.at[0])
+    h_copy = pltpu.make_async_copy(h_ref, h_out, sem.at[1])
+    grad_copy.start()
+    h_copy.start()
+    blank = bias_ref[...].astype(jnp.bfloat16).astype(jnp.float32)
+    value = jnp.where(kept_ref[...] >= 0, picked_ref[...].astype(jnp.float32), blank)
+    recon[...] = value.astype(jnp.bfloat16)
+    recon_copy = pltpu.make_async_copy(recon, recon_out, sem.at[2])
+    recon_copy.start()
+    error[...] = (value - h_ref[...].astype(jnp.float32)).astype(jnp.bfloat16)
+    error_copy = pltpu.make_async_copy(error, error_out, sem.at[3])
+    error_copy.start()
+    for copy in (grad_copy, h_copy, recon_copy, error_copy):
+        copy.wait()
+
+
+def run_finish(harvested, picked, slot_ids, dec_bias, dec_grad):
+    rows = jax.ShapeDtypeStruct(harvested.shape, jnp.bfloat16)
+    vmem = pl.BlockSpec(memory_space=pltpu.VMEM)
+    hbm = pl.BlockSpec(memory_space=pl.ANY)
+    return pl.pallas_call(
+        finish_kernel,
+        out_shape=(rows, rows, rows, jax.ShapeDtypeStruct(dec_grad.shape, jnp.bfloat16)),
+        in_specs=[vmem] * 4 + [hbm],
+        out_specs=(hbm,) * 4,
+        scratch_shapes=[
+            pltpu.VMEM(harvested.shape, jnp.bfloat16),
+            pltpu.VMEM(harvested.shape, jnp.bfloat16),
+            pltpu.SemaphoreType.DMA((4,)),
+        ],
+        compiler_params=pltpu.CompilerParams(vmem_limit_bytes=16 * 2**20),
+    )(harvested, picked, slot_ids[:, None], dec_bias[None, :], dec_grad)
 
 
 def shards(
@@ -462,15 +540,12 @@
     slot_here = slot_ids[0]
     kept_token = slot_here >= 0
     slot_count = experts_all * capacity
-    target = jnp.where(kept_token, expert_here * capacity + slot_here, slot_count)
+    target = jnp.where(kept_token, place_of(expert_here) * capacity + slot_here, slot_count)
     picked_rows, dec_grad = run_experts(
         harvested, target, enc_weight[0], enc_bias[0], dec_weight[0], dec_bias, slot_count
     )
-    reconstruction = jnp.where(
-        kept_token[:, None], picked_rows, dec_bias.astype(jnp.bfloat16)[None, :]
-    )
-    error_rows = (reconstruction.astype(jnp.float32) - harvested.astype(jnp.float32)).astype(
-        jnp.bfloat16
+    harvested, reconstruction, error_rows, dec_grad = run_finish(
+        harvested, picked_rows, slot_here, dec_bias, dec_grad
     )
     return (harvested[None], reconstruction[None], error_rows[None], dec_grad[None])
 

time: 146 us -> 145 us (level)
  the two profiles are of different devices: /device:TPU:1 before, /device:TPU:73 now
where the time goes in v3:
time: 145 us; the launch traced here: 144 us
  Pallas kernels  133 us (92%)
  local copies, waits for them, and re-layouts  8.69 us (6%)
    pallas_call x1, Pallas kernels, run_attention(): pl.pallas_call(attention_kernel, out_shape=jax.ShapeDtypeStruct((tokens,...  66.4 us
    pallas_call x1, Pallas kernels, run_experts(): pl.pallas_call(experts_kernel, out_shape=(jax.ShapeDtypeStruct((tokens, w...  64.1 us
    unnamed x14, local copies, waits for them, and re-layouts  6.23 us

profile of v3, /device:TPU:73, one launch (start us, length us, event | category | flops | bytes accessed | tf_op | source)
XLA Modules:
  0.0 144.1 jit_solution(4950869520303994438)
XLA Ops:
  0.7 0.8 dynamic-slice_bitcast_fusion
  1.4 0.8 compare_select_fusion.10.row_ref
  2.2 0.1 copy.15.doc_col
  2.3 0.8 copy.16.kept_ref
  3.1 0.8 copy.17
  3.9 0.5 fusion.18.col_ref
  4.4 0.0 copy-start
  4.4 1.4 copy-done
  5.8 0.0 copy-start.1
  5.8 0.9 copy-done.1
  6.7 0.0 copy-start.2
  6.7 0.9 copy-done.2
  7.6 0.0 copy-start.3
  7.6 0.9 copy-done.3
  8.5 0.0 copy-start.5
  8.5 0.7 copy-done.5
  9.2 66.4 %shard_map.138.h_ref = bf16[192,2048]{1,0:T(8,128)(2,1)S(1)} custom-call(bf16[192,4096]{1,0:T(8,128)(2,1)S(1)} %bitcast.14, bf16[192,512]{1,0:T(8,128)(2,1)S(1)} %bitcast.15, bf16[192,512]{1,0:T(8,128)(2,1)S(1)} %bitcast.16, s32[192,1]{1,0:T(8,128)S(1)} %copy.15.doc_col, s32[1,1536]{1,0:T(1,128)S(1)} %copy-done.5, bf16[32,2048]{1,0:T(8,128)(2,1)S(1)} %copy-done.3), custom_call_target="tpu_custom_call" | custom-call | tf_op jit(solution)/shard_map/pallas_call | solution.py:222
  75.7 0.0 copy-start.4
  75.7 0.7 copy-done.4
  76.4 0.0 copy-start.6
  76.4 0.7 copy-done.6
  77.0 64.1 %shard_map.139 = (bf16[192,2048]{1,0:T(8,128)(2,1)S(1)}, bf16[1024,2048]{1,0:T(8,128)(2,1)S(1)}) custom-call(bf16[192,2048]{1,0:T(8,128)(2,1)S(1)} %shard_map.138.h_ref, s32[1,192]{1,0:T(1,128)S(1)} %compare_select_fusion.10.row_ref, s32[192,1]{1,0:T(8,128)S(1)} %fusion.18.col_ref, bf16[2048,1024]{1,0:T(8,128)(2,1)} %bitcast.19, f32[1,1024]{1,0:T(1,128)S(1)} %copy-done.6, ...), custom_call_target="tpu_custom_call" | custom-call | tf_op jit(solution)/shard_map/pallas_call | solution.py:445
  141.2 2.8 %shard_map.140 = (bf16[192,2048]{1,0:T(8,128)(2,1)}, bf16[192,2048]{1,0:T(8,128)(2,1)}, bf16[192,2048]{1,0:T(8,128)(2,1)}, bf16[1024,2048]{1,0:T(8,128)(2,1)}) custom-call(bf16[192,2048]{1,0:T(8,128)(2,1)S(1)} %shard_map.138.h_ref, bf16[192,2048]{1,0:T(8,128)(2,1)S(1)} %get-tuple-element.10.picked_ref, s32[192,1]{1,0:T(8,128)S(1)} %copy.16.kept_ref, ...), custom_call_target="tpu_custom_call" | custom-call | tf_op jit(solution)/shard_map/pallas_call | solution.py:498
Async XLA Ops:
  4.4 1.4 copy-start
  5.8 0.9 copy-start.1
  6.7 0.9 copy-start.2
  7.6 0.9 copy-start.3
  8.5 0.7 copy-start.5
  75.7 0.7 copy-start.4
  76.4 0.7 copy-start.6

commit v4 on v3

v4 whole, which is shorter than its diff:
```python
import math

import jax
import jax.numpy as jnp
from jax import lax
from jax.experimental import pallas as pl
from jax.experimental.pallas import tpu as pltpu
from jax.sharding import PartitionSpec as P

HEAD_DIMENSION = 128
MESH = pl.DeviceIdType.MESH
TILE = 128
EMPTY = 1e30
PARTS = ((0, 384), (384, 256), (640, 384))
ORDERS = ("xyz", "yzx", "xzy")


def attention_part(
    q_hbm, k_hbm, v_hbm, doc_hbm, w_hbm,
    out_ref,
    doc_row, queries, kv, w_a, w_b, w_c, attended, bias, result, half_in,
    send_sem, recv_sem, local_sem,
):
    s, p = lax.axis_index("seq"), lax.axis_index("exp")
    place = {"x": s // 2, "y": p // 4, "z": lax.rem(p, 4)}
    core = lax.rem(s, 2)
    tokens = queries.shape[0]
    kv_width = k_hbm.shape[1]
    span = kv.shape[0] * tokens
    half = out_ref.shape[1] // 2
    heads = queries.shape[1] // HEAD_DIMENSION
    group = heads // (kv_width // HEAD_DIMENSION)
    scale = math.log2(math.e) / math.sqrt(HEAD_DIMENSION)
    parts = (w_a, w_b, w_c)
    partner = (2 * place["x"] + 1 - core, p)

    def beside(axis, step):
        at = dict(place)
        at[axis] = lax.rem(at[axis] + step + 4, 4)
        return (2 * at["x"] + core, 4 * at["y"] + at["z"])

    peers = [partner] + [beside(axis, step) for axis in "xyz" for step in (1, -1)]
    barrier = pltpu.get_barrier_semaphore()
    for peer in peers:
        pl.semaphore_signal(barrier, inc=1, device_id=peer, device_id_type=MESH)

    started = []

    def send(src, dst, peer):
        copy = pltpu.make_async_remote_copy(
            src_ref=src,
            dst_ref=dst,
            send_sem=send_sem.at[len(started)],
            recv_sem=recv_sem.at[len(started)],
            device_id=peer,
            device_id_type=MESH,
        )
        started.append(copy)
        copy.start()
        return copy

    def arrive(copies):
        for copy in copies:
            copy.wait_recv()

    own = [
        (k_hbm, kv.at[s, :, pl.ds(0, kv_width)]),
        (v_hbm, kv.at[s, :, pl.ds(kv_width, kv_width)]),
    ]
    for (first, wide), buffer in zip(PARTS, parts):
        columns = pl.ds(pl.multiple_of(core * half + first, TILE), wide)
        own.append((w_hbm.at[:, columns], buffer.at[place["x"], core, place["y"], place["z"]]))
    own.append((doc_hbm, doc_row))
    own.append((q_hbm, queries))
    own = [pltpu.make_async_copy(a, b, local_sem.at[i]) for i, (a, b) in enumerate(own)]
    for copy in own:
        copy.start()
    own[0].wait()
    own[1].wait()
    pl.semaphore_wait(barrier, len(peers))

    kv_near = [send(kv.at[s], kv.at[s], beside("x", step)) for step in (1, -1)]
    kv_own_pair = send(kv.at[s], kv.at[s], partner)
    w_pair = []
    for (first, wide), buffer in zip(PARTS, parts):
        columns = pl.ds(pl.multiple_of((1 - core) * half + first, TILE), wide)
        w_pair.append(
            send(
                w_hbm.at[:, columns],
                buffer.at[place["x"], core, place["y"], place["z"]],
                partner,
            )
        )

    def view(part, offsets, row=None):
        at = {}
        for axis, offset in zip(ORDERS[part], offsets):
            if offset is None:
                at[axis] = pl.ds(0, 4)
            else:
                at[axis] = pl.ds(lax.rem(place[axis] + offset + 4, 4), 1)
        rows = pl.ds(0, 2) if row is None else pl.ds(row, 1)
        return parts[part].at[at["x"], rows, at["y"], at["z"]]

    def near(stage, offsets):
        copies = []
        for part in range(3):
            block = view(part, offsets)
            for step in (1, -1):
                copies.append(send(block, block, beside(ORDERS[part][stage], step)))
        return copies

    def far(stage, offsets):
        copies = []
        for part in range(3):
            for step, row in ((1, 0), (-1, 1)):
                at = offsets[:stage] + (-step,) + offsets[stage + 1 :]
                block = view(part, at, row)
                copies.append(send(block, block, beside(ORDERS[part][stage], step)))
        return copies

    def attend(first, last, blocks):
        keys = blocks * tokens

        def one_head(h, carry):
            g = h // group
            q_at = pl.ds(pl.multiple_of(h * HEAD_DIMENSION, HEAD_DIMENSION), HEAD_DIMENSION)
            k_at = pl.ds(pl.multiple_of(g * HEAD_DIMENSION, HEAD_DIMENSION), HEAD_DIMENSION)
            v_at = pl.ds(
                pl.multiple_of(kv_width + g * HEAD_DIMENSION, HEAD_DIMENSION), HEAD_DIMENSION
            )
            key_part = kv[:blocks, :, k_at].reshape(keys, HEAD_DIMENSION)
            value_part = kv[:blocks, :, v_at].reshape(keys, HEAD_DIMENSION)
            scores = lax.dot_general(
                queries[:, q_at], key_part, (((1,), (1,)), ((), ())),
                preferred_element_type=jnp.float32,
            )
            scores = scores + bias[:, :keys]
            highest = jnp.max(scores, axis=1, keepdims=True)
            weights = jnp.exp2((scores - highest) * scale)
            total = jnp.sum(weights, axis=1, keepdims=True)
            mixed = jnp.dot(
                weights.astype(jnp.bfloat16), value_part, preferred_element_type=jnp.float32
            )
            attended[core, :, q_at] = (mixed / total).astype(jnp.bfloat16)
            return carry

        lax.fori_loop(first, last, one_head, 0)

    def attend_some(quarter):
        first, last = quarter * heads // 4, (quarter + 1) * heads // 4
        for chips in range(1, 5):

            @pl.when(place["x"] == chips - 1)
            def _():
                attend(first, last, 2 * chips)

        columns = pl.ds(first * HEAD_DIMENSION, (last - first) * HEAD_DIMENSION)
        piece = attended.at[core, :, columns]
        return send(piece, piece, partner)

    arrive(w_pair)
    for copy in own[2:5]:
        copy.wait()
    near_1 = near(0, (0, 0, 0))
    near_2 = near(1, (0, 0, 0))
    near_3 = near(2, (0, 0, 0))
    own[5].wait()
    rows_at = s * tokens + lax.broadcasted_iota(jnp.int32, (tokens, span), 0)
    keys_at = lax.broadcasted_iota(jnp.int32, (tokens, span), 1)
    doc_all = doc_row[...].astype(jnp.float32)
    doc_mine = jnp.sum(jnp.where(rows_at == keys_at, doc_all, 0.0), axis=1, keepdims=True)
    visible = (rows_at >= keys_at) & (doc_mine == doc_all)
    bias[...] = jnp.where(visible, 0.0, -EMPTY)
    own[6].wait()
    arrive([kv_own_pair])
    arrive(near_1)
    far_1 = far(0, (None, 0, 0))
    for offset in (-1, 1):
        near_2 += near(1, (offset, 0, 0))
        near_3 += near(2, (offset, 0, 0))
    arrive(far_1)
    near_2 += near(1, (2, 0, 0))
    near_3 += near(2, (2, 0, 0))
    arrive(kv_near)
    kv_far = []
    for step, first in ((1, 0), (-1, tokens // 2)):
        origin = 2 * lax.rem(place["x"] - step + 4, 4) + core
        piece = kv.at[origin, pl.ds(first, tokens // 2)]
        kv_far.append(send(piece, piece, beside("x", step)))
    kv_pair = []
    for step in (1, -1):
        piece = kv.at[2 * lax.rem(place["x"] - step + 4, 4) + core]
        kv_pair.append(send(piece, piece, partner))
    arrive(near_2)
    far_2 = far(1, (None, None, 0))
    near_3b = near(2, (None, -1, 0)) + near(2, (None, 1, 0))
    arrive(kv_far)
    piece = kv.at[2 * lax.rem(place["x"] + 2, 4) + core]
    kv_pair.append(send(piece, piece, partner))
    arrive(far_2)
    near_3c = near(2, (None, 2, 0))
    arrive(kv_pair)
    across = [attend_some(0)]
    arrive(near_3)
    far_3 = far(2, (None, 0, None))
    across.append(attend_some(1))
    arrive(near_3b)
    far_3 += far(2, (None, -1, None)) + far(2, (None, 1, None))
    across.append(attend_some(2))
    arrive(near_3c)
    far_3 += far(2, (None, 2, None))
    across.append(attend_some(3))
    arrive(across)
    arrive(far_3)

    rows = attended.shape[1] * 2
    for (first, wide), buffer in zip(PARTS, parts):
        both = jnp.dot(
            attended[...].reshape(rows, heads * HEAD_DIMENSION),
            buffer[...].reshape(heads * HEAD_DIMENSION, wide),
            preferred_element_type=jnp.float32,
        )
        result[:, :, first : first + wide] = both.astype(jnp.bfloat16).reshape(2, tokens, wide)
    back = send(result.at[1 - core], half_in, partner)
    out_ref[:, pl.ds(pl.multiple_of(core * half, half), half)] = result[core]
    arrive([back])
    out_ref[:, pl.ds(pl.multiple_of((1 - core) * half, half), half)] = half_in[...]
    for copy in started:
        copy.wait_send()


GROUPS = 2
VMEM_MIB = 60


def widen(src, wide, first, rows):
    def step(i, carry):
        at = pl.ds(pl.multiple_of(first + i * 384, 384), 384)
        wide[at, :] = src[at, :].astype(jnp.float32)
        return carry

    lax.fori_loop(0, rows // 384, step, 0)


def narrow(wide, dst, first, rows):
    def step(i, carry):
        at = pl.ds(pl.multiple_of(first + i * 384, 384), 384)
        dst[at, :] = wide[at, :].astype(jnp.bfloat16)
        return carry

    lax.fori_loop(0, rows // 384, step, 0)


def peer_at(group, i, sign):
    s, p = lax.axis_index("seq"), lax.axis_index("exp")
    i = i + group * (lax.axis_size("seq") * lax.axis_size("exp") // GROUPS)
    turn, i = i // 32, lax.rem(i, 32)
    along_x, along_y, across = i // 8, lax.rem(i // 2, 4), lax.rem(i, 2)
    along_z = lax.rem(turn + 8 - along_x - along_y, 4)
    x = lax.rem(s // 2 + sign * along_x + 4, 4)
    y = lax.rem(p // 4 + sign * along_y + 4, 4)
    z = lax.rem(lax.rem(p, 4) + sign * along_z + 4, 4)
    return (2 * x + lax.rem(s + across, 2), 4 * y + z)


def place_of(expert):
    s, p = lax.axis_index("seq"), lax.axis_index("exp")
    to_s, to_p = expert >> 4, expert & 15
    along_x = ((to_s >> 1) - s // 2) & 3
    along_y = ((to_p >> 2) - p // 4) & 3
    along_z = (to_p - p) & 3
    across = (to_s + s) & 1
    turn = (along_x + along_y + along_z) & 3
    return turn * 32 + along_x * 8 + along_y * 2 + across


def exchange_start(group, sign, src, dst, send_sem, recv_sem, own_sem, chunk):
    members = src.shape[0] // chunk // GROUPS

    def step(i, carry):
        at = pl.ds(pl.multiple_of((group * members + i) * chunk, chunk), chunk)
        pltpu.make_async_remote_copy(
            src_ref=src.at[at],
            dst_ref=dst.at[at],
            send_sem=send_sem.at[group],
            recv_sem=recv_sem.at[group],
            device_id=peer_at(group, i, sign),
            device_id_type=MESH,
        ).start()
        return carry

    if group == 0:
        own = pl.ds(0, chunk)
        pltpu.make_async_copy(src.at[own], dst.at[own], own_sem).start()
    lax.fori_loop(1 if group == 0 else 0, members, step, 0)


def group_rows(group, src, chunk):
    members = src.shape[0] // chunk // GROUPS
    first = group * members + (1 if group == 0 else 0)
    return pl.ds(first * chunk, ((group + 1) * members - first) * chunk)


def exchange_wait(group, src, dst, recv_sem, own_sem, chunk):
    if group == 0:
        own = pl.ds(0, chunk)
        pltpu.make_async_copy(src.at[own], dst.at[own], own_sem).wait()
    at = group_rows(group, src, chunk)
    pltpu.make_async_copy(src.at[at], dst.at[at], recv_sem.at[group]).wait()


def exchange_sent(group, src, dst, send_sem, chunk):
    at = group_rows(group, src, chunk)
    pltpu.make_async_copy(src.at[at], dst.at[at], send_sem.at[group]).wait()


def experts_load(hbm, vmem, sem):
    copies = [pltpu.make_async_copy(a, b, sem.at[i]) for i, (a, b) in enumerate(zip(hbm, vmem))]
    for copy in copies:
        copy.start()
    return copies


def experts_part(
    loads, h_ref, recon_out, error_out, grad_out, out_sem,
    encw, decw, expert_row, slot_row, encb_ref, decb_ref, picks,
    wide, send, recv, back, ret, slot_rows, centered, latent, gated, residue,
    own_sem, send_sem, recv_sem, send_back_sem, recv_back_sem,
):
    tokens, width = h_ref.shape
    slots = slot_rows.shape[0]
    latents = latent.shape[1]
    lanes = width // TILE
    members = lax.axis_size("seq") * lax.axis_size("exp") // GROUPS
    chunk = slots // (members * GROUPS) * lanes
    part_slots = slots // GROUPS
    part_rows = part_slots * lanes
    enc_copy, dec_copy, *small = loads
    for copy in small:
        copy.wait()
    capacity = slots // (members * GROUPS)
    target = jnp.where(
        slot_row[...] >= 0, place_of(expert_row[...]) * capacity + slot_row[...], slots
    )

    for group in range(GROUPS):
        first = group * part_rows
        place = lax.broadcasted_iota(jnp.int32, (part_slots, tokens), 0) + group * part_slots
        pick = jnp.where(place == target, 1.0, 0.0)
        free = (1.0 - jnp.sum(pick, axis=1, keepdims=True)) * EMPTY
        pick = pick.astype(jnp.bfloat16)
        picks[group * part_slots : (group + 1) * part_slots, :] = pick
        for n in range(lanes // 2):
            rows = jnp.dot(
                pick,
                h_ref[:, 2 * n * TILE : 2 * (n + 1) * TILE],
                preferred_element_type=jnp.float32,
            )
            if n == 0:
                rows = rows + free
            wide[pl.ds(first + 2 * n, part_slots, stride=lanes), :] = rows[:, :TILE]
            wide[pl.ds(first + 2 * n + 1, part_slots, stride=lanes), :] = rows[:, TILE:]
        narrow(wide, send, first, part_rows)
        exchange_start(group, 1, send, recv, send_sem, recv_sem, own_sem.at[0], chunk)

    enc_copy.wait()
    dec_copy.wait()
    for group in range(GROUPS):
        first = group * part_rows
        mine = slice(group * part_slots, (group + 1) * part_slots)
        exchange_wait(group, send, recv, recv_sem, own_sem.at[0], chunk)
        widen(recv, wide, first, part_rows)
        live = wide[pl.ds(first, part_slots, stride=lanes), :][:, :1] < 0.5 * EMPTY
        for c in range(lanes):
            at = slice(c * TILE, (c + 1) * TILE)
            part = wide[pl.ds(first + c, part_slots, stride=lanes), :]
            if c < 2:
                part = jnp.where(live, part, 0.0)
            slot_rows[mine, at] = part.astype(jnp.bfloat16)
            centered[mine, at] = (part - decb_ref[:, at]).astype(jnp.bfloat16)
        for n in range(latents // 256):
            at = slice(n * 256, (n + 1) * 256)
            pre = jnp.dot(centered[mine, :], encw[:, at], preferred_element_type=jnp.float32)
            act = jnp.maximum(pre + encb_ref[:, at], 0.0)
            latent[mine, at] = act.astype(jnp.bfloat16)
            gated[mine, at] = jnp.where(live, act, 0.0).astype(jnp.bfloat16)
        for n in range(lanes // 2):
            at = slice(2 * n * TILE, 2 * (n + 1) * TILE)
            rebuilt = jnp.dot(latent[mine, :], decw[:, at], preferred_element_type=jnp.float32)
            rebuilt = (rebuilt + decb_ref[:, at]).astype(jnp.bfloat16).astype(jnp.float32)
            error = rebuilt - slot_rows[mine, at].astype(jnp.float32)
            residue[mine, at] = error.astype(jnp.bfloat16)
            wide[pl.ds(first + 2 * n, part_slots, stride=lanes), :] = rebuilt[:, :TILE]
            wide[pl.ds(first + 2 * n + 1, part_slots, stride=lanes), :] = rebuilt[:, TILE:]
        narrow(wide, back, first, part_rows)
        exchange_start(group, -1, back, ret, send_back_sem, recv_back_sem, own_sem.at[1], chunk)

    outs = []
    for n in range(latents // 256):
        at = slice(n * 256, (n + 1) * 256)
        decw[at, :] = lax.dot_general(
            gated[:, at], residue[...], (((0,), (0,)), ((), ())),
            preferred_element_type=jnp.float32,
        ).astype(jnp.bfloat16)
        rows = pl.ds(n * 256, 256)
        outs.append(pltpu.make_async_copy(decw.at[rows], grad_out.at[rows], out_sem.at[3 + n]))
        outs[-1].start()

    def gather_back(rows):
        return lax.dot_general(
            picks[...], rows, (((0,), (0,)), ((), ())), preferred_element_type=jnp.float32
        )

    kept = gather_back(jnp.ones((slots, TILE), jnp.bfloat16))[:, :1] > 0.5
    for group in range(GROUPS):
        first = group * part_rows
        mine = slice(group * part_slots, (group + 1) * part_slots)
        exchange_wait(group, back, ret, recv_back_sem, own_sem.at[1], chunk)
        widen(ret, wide, first, part_rows)
        for c in range(lanes):
            slot_rows[mine, c * TILE : (c + 1) * TILE] = wide[
                pl.ds(first + c, part_slots, stride=lanes), :
            ].astype(jnp.bfloat16)
    for n in range(width // 256):
        at = slice(n * 256, (n + 1) * 256)
        rows = jnp.where(kept, gather_back(slot_rows[:, at]), decb_ref[:, at]).astype(jnp.bfloat16)
        centered[:tokens, at] = rows
        error = rows.astype(jnp.float32) - h_ref[:, at].astype(jnp.float32)
        centered[tokens : 2 * tokens, at] = error.astype(jnp.bfloat16)
    for i, out in enumerate((recon_out, error_out)):
        rows = centered.at[pl.ds(i * tokens, tokens)]
        outs.append(pltpu.make_async_copy(rows, out, out_sem.at[1 + i]))
        outs[-1].start()
    for copy in outs:
        copy.wait()
    for group in range(GROUPS):
        exchange_sent(group, send, recv, send_sem, chunk)
        exchange_sent(group, back, ret, send_back_sem, chunk)


def whole_kernel(
    q_hbm, k_hbm, v_hbm, doc_hbm, w_hbm,
    expert_hbm, slot_hbm, encw_hbm, encb_hbm, decw_hbm, decb_hbm,
    h_out, recon_out, error_out, grad_out, *scratch,
):
    first, second = scratch[:13], scratch[13:-3]
    load_sem, out_sem, h_ref = scratch[-3:]
    loads = experts_load(
        (encw_hbm, decw_hbm, expert_hbm, slot_hbm, encb_hbm, decb_hbm), second[:6], load_sem
    )
    attention_part(q_hbm, k_hbm, v_hbm, doc_hbm, w_hbm, h_ref, *first)
    h_copy = pltpu.make_async_copy(h_ref, h_out, out_sem.at[0])
    h_copy.start()
    experts_part(loads, h_ref, recon_out, error_out, grad_out, out_sem, *second)
    h_copy.wait()


def run_whole(
    query, key, value, doc_all, out_weight, experts, slot_ids, enc_weight, enc_bias, dec_weight,
    dec_bias, seq_groups, slots,
):
    tokens, q_width = query.shape
    kv_width = key.shape[1]
    span = tokens * seq_groups
    rows, width = out_weight.shape
    latents = enc_bias.shape[1]
    lanes = width // TILE
    hbm = pl.BlockSpec(memory_space=pl.ANY)
    dma = pltpu.SemaphoreType.DMA
    copies = 128

    def half(*shape):
        return pltpu.VMEM(shape, jnp.bfloat16)

    def full(*shape):
        return pltpu.VMEM(shape, jnp.float32)

    return pl.pallas_call(
        whole_kernel,
        out_shape=(
            *[jax.ShapeDtypeStruct((tokens, width), jnp.bfloat16)] * 3,
            jax.ShapeDtypeStruct((latents, width), jnp.bfloat16),
        ),
        in_specs=[hbm] * 11,
        out_specs=(hbm,) * 4,
        scratch_shapes=[
            pltpu.VMEM((1, span), jnp.int32),
            half(tokens, q_width),
            half(seq_groups, tokens, 2 * kv_width),
            *[half(4, 2, 4, 4, rows, wide) for _, wide in PARTS],
            half(2, tokens, q_width),
            full(tokens, span),
            half(2, tokens, width // 2),
            half(tokens, width // 2),
            dma((copies,)),
            dma((copies,)),
            dma((7,)),
            half(width, latents),
            half(latents, width),
            pltpu.VMEM((1, tokens), jnp.int32),
            pltpu.VMEM((1, tokens), jnp.int32),
            full(1, latents),
            full(1, width),
            half(slots, tokens),
            full(slots * lanes, TILE),
            *[half(slots * lanes, TILE)] * 4,
            half(slots, width),
            half(slots, width),
            half(slots, latents),
            half(slots, latents),
            half(slots, width),
            dma((2,)),
            *[dma((GROUPS,))] * 4,
            dma((6,)),
            dma((3 + latents // 256,)),
            half(tokens, width),
        ],
        compiler_params=pltpu.CompilerParams(
            collective_id=0, has_side_effects=True, vmem_limit_bytes=VMEM_MIB * 2**20
        ),
    )(
        query, key, value, doc_all, out_weight, experts, slot_ids, enc_weight, enc_bias,
        dec_weight, dec_bias[None, :],
    )


def finish_kernel(*refs):
    sources, targets, held, sems = refs[:4], refs[4:8], refs[8:12], refs[12:]
    pairs = []
    for source, hold, target in zip(sources, held, targets):
        rows = source.shape[0]
        for first in range(0, rows, 192):
            at = pl.ds(first, min(192, rows - first))
            i = len(pairs)
            pairs.append(
                (
                    pltpu.make_async_copy(source.at[at], hold.at[at], sems[0].at[i]),
                    pltpu.make_async_copy(hold.at[at], target.at[at], sems[1].at[i]),
                )
            )
            pairs[-1][0].start()
    for fetch, store in pairs:
        fetch.wait()
        store.start()
    for fetch, store in pairs:
        store.wait()


def run_finish(*arrays):
    hbm = pl.BlockSpec(memory_space=pl.ANY)
    return pl.pallas_call(
        finish_kernel,
        out_shape=tuple(jax.ShapeDtypeStruct(a.shape, a.dtype) for a in arrays),
        in_specs=[hbm] * 4,
        out_specs=(hbm,) * 4,
        scratch_shapes=[
            *[pltpu.VMEM(a.shape, a.dtype) for a in arrays],
            pltpu.SemaphoreType.DMA((16,)),
            pltpu.SemaphoreType.DMA((16,)),
        ],
        compiler_params=pltpu.CompilerParams(vmem_limit_bytes=VMEM_MIB * 2**20),
    )(*arrays)


def shards(
    query_rows,
    key_rows,
    value_matrix,
    doc_ids,
    out_weight,
    enc_weight,
    enc_bias,
    dec_weight,
    dec_bias,
    expert_ids,
    slot_ids,
):
    local_tokens = query_rows.shape[1]
    seq_groups = lax.axis_size("seq")
    experts_all = enc_weight.shape[0] * seq_groups * lax.axis_size("exp")
    slot_count = 2 * local_tokens // experts_all * experts_all
    outputs = run_whole(
        query_rows[0], key_rows[0], value_matrix[0], doc_ids, out_weight, expert_ids, slot_ids,
        enc_weight[0], enc_bias, dec_weight[0], dec_bias, seq_groups, slot_count,
    )
    harvested, reconstruction, error_rows, dec_grad = run_finish(*outputs)
    return (harvested[None], reconstruction[None], error_rows[None], dec_grad[None])


def solution(mesh):
    return jax.shard_map(
        shards,
        mesh=mesh,
        in_specs=(
            P("exp", "seq", None),
            P("exp", "seq", None),
            P("exp", "seq", None),
            P("exp", None),
            P(("seq", "exp"), None),
            P(("seq", "exp"), None, None),
            P(("seq", "exp"), None),
            P(("seq", "exp"), None, None),
            P(),
            P("exp", "seq"),
            P("exp", "seq"),
        ),
        out_specs=(
            P("exp", "seq", None),
            P("exp", "seq", None),
            P("exp", "seq", None),
            P(("seq", "exp"), None, None),
        ),
        check_vma=False,
    )
```

time: 145 us -> 125 us (0.86)
  the two profiles are of different devices: /device:TPU:73 before, /device:TPU:1 now
where the time goes in v4:
time: 125 us; the launch traced here: 123 us
  Pallas kernels  122 us (98%)
    pallas_call x1, Pallas kernels, run_whole(): pl.pallas_call(whole_kernel, out_shape=(*[jax.ShapeDtypeStruct((tokens, w...  117 us
    pallas_call x1, Pallas kernels, run_finish(): pl.pallas_call(finish_kernel, out_shape=tuple((jax.ShapeDtypeStruct(a.sha...  5.71 us

profile of v4, /device:TPU:1, one launch (start us, length us, event | category | flops | bytes accessed | tf_op | source)
XLA Modules:
  0.0 123.2 jit_solution(13042446238390267782)
XLA Ops:
  0.6 116.7 %shard_map.138 = (bf16[192,2048]{1,0:T(8,128)(2,1)}, bf16[192,2048]{1,0:T(8,128)(2,1)}, bf16[192,2048]{1,0:T(8,128)(2,1)}, bf16[1024,2048]{1,0:T(8,128)(2,1)}) custom-call(bf16[192,4096]{1,0:T(8,128)(2,1)} %bitcast.12, bf16[192,512]{1,0:T(8,128)(2,1)} %bitcast.13, bf16[192,512]{1,0:T(8,128)(2,1)} %bitcast.14, s32[1,1536]{1,0:T(1,128)} %doc_hbm.1, ...), custom_call_target="tpu_custom_call" | custom-call | tf_op jit(solution)/shard_map/pallas_call | solution.py:479
  117.3 5.7 %shard_map.139 = (bf16[192,2048]{1,0:T(8,128)(2,1)}, bf16[192,2048]{1,0:T(8,128)(2,1)}, bf16[192,2048]{1,0:T(8,128)(2,1)}, bf16[1024,2048]{1,0:T(8,128)(2,1)}) custom-call(bf16[192,2048]{1,0:T(8,128)(2,1)} %get-tuple-element.12.refs_0_, bf16[192,2048]{1,0:T(8,128)(2,1)} %get-tuple-element.13.refs_1_, bf16[192,2048]{1,0:T(8,128)(2,1)} %get-tuple-element.14.refs_2_, ...), custom_call_target="tpu_custom_call" | custom-call | tf_op jit(solution)/shard_map/pallas_call | solution.py:552
